TPU v7x, 512 devices: a whole 4x4x16 slice. The times are simulated.
512 devices in a mesh: img: 16 (over y, z_lo), txt: 32 (over z_hi, x, core).
Axes of the slice: x: 4, y: 4, z: 16 (z_hi: 4, z_lo: 4; z = z_hi * 4 + z_lo), core: 2. Of those that a mesh axis runs over, the one named last changes fastest.
Arguments:
- images: bfloat16 [16384, 1024], P(('img', 'txt')), may hold values from -2 to 2
- texts: bfloat16 [16, 1024, 1024], P('img', 'txt'), may hold values from -2 to 2
Outputs:
- contrastive_loss: float32 [], replicated
- grad_images: bfloat16 [16384, 1024], P(('img', 'txt'))
- grad_texts: bfloat16 [16, 1024, 1024], P('img', 'txt')
All inputs are finite; a program needn't handle non-finite values.
Results may differ from a plain program's by a relative error of at most 0.02.
Values may be sent and summed in bfloat16 or wider, within the bound.
A program may use at most 64 MiB of HBM per device.

v0:
```python
import jax
import jax.numpy as jnp
from jax import lax
from jax.sharding import PartitionSpec as P

LOGIT_SCALE = 1.0 / 0.07


def per_device(images, texts):
    img_count = lax.axis_size("img")
    txt_count = lax.axis_size("txt")
    own_rows = images.shape[0]
    own_texts = texts.shape[1]
    embed_width = images.shape[1]
    pair_count = own_rows * img_count * txt_count
    image_block = lax.all_gather(images, "txt", axis=0, tiled=True)
    text_block = lax.all_gather(texts, "img", axis=0, tiled=True).reshape(
        img_count * own_texts, embed_width
    )
    block_rows = image_block.shape[0]
    block_cols = text_block.shape[0]
    row_first = lax.axis_index("img") * block_rows
    col_first = lax.axis_index("txt") * block_cols
    logits = LOGIT_SCALE * lax.dot_general(
        image_block, text_block, (((1,), (1,)), ((), ())), preferred_element_type=jnp.float32
    )
    row_local = jnp.max(logits, axis=1)
    col_local = jnp.max(logits, axis=0)
    row_peak = lax.pmax(row_local, "txt")
    col_peak = lax.pmax(col_local, "img")
    row_total = lax.psum(jnp.sum(jnp.exp(logits - row_peak[:, None]), axis=1), "txt")
    col_total = lax.psum(jnp.sum(jnp.exp(logits - col_peak[None, :]), axis=0), "img")
    row_lse = row_peak + jnp.log(row_total)
    col_lse = col_peak + jnp.log(col_total)
    row_ids = row_first + lax.broadcasted_iota(jnp.int32, (block_rows, 1), 0)
    col_ids = col_first + lax.broadcasted_iota(jnp.int32, (1, block_cols), 1)
    diagonal = (row_ids == col_ids).astype(jnp.float32)
    own_row_lse = lax.dynamic_slice_in_dim(row_lse, lax.axis_index("txt") * own_rows, own_rows)
    own_col_lse = lax.dynamic_slice_in_dim(col_lse, lax.axis_index("img") * own_texts, own_texts)
    local_term = jnp.sum(own_row_lse) + jnp.sum(own_col_lse) - 2.0 * jnp.sum(logits * diagonal)
    contrastive_loss = lax.psum(local_term, ("img", "txt")) / (2.0 * pair_count)
    weights = (
        0.5
        * LOGIT_SCALE
        * (jnp.exp(logits - row_lse[:, None]) + jnp.exp(logits - col_lse[None, :]) - 2.0 * diagonal)
    ).astype(jnp.bfloat16)
    partial_image = jnp.dot(weights, text_block, preferred_element_type=jnp.float32)
    partial_text = lax.dot_general(
        weights, image_block, (((0,), (0,)), ((), ())), preferred_element_type=jnp.float32
    )
    grad_image = lax.psum_scatter(
        partial_image.astype(jnp.bfloat16), "txt", scatter_dimension=0, tiled=True
    )
    grad_text = lax.psum_scatter(
        partial_text.astype(jnp.bfloat16), "img", scatter_dimension=0, tiled=True
    )
    return (contrastive_loss, grad_image, grad_text.reshape(1, own_texts, embed_width))


def solution(mesh):
    in_specs = (P(("img", "txt"), None), P("img", "txt", None))
    out_specs = (P(), P(("img", "txt"), None), P("img", "txt", None))
    return jax.shard_map(
        per_device, mesh=mesh, in_specs=in_specs, out_specs=out_specs, check_vma=False
    )
```

profile of v0, /device:TPU:24, one launch (start us, length us, event | category | flops | bytes accessed | tf_op | source)
XLA Modules:
  0.0 653.0 jit_solution(2751876920050075185)
XLA Ops:
  7.2 0.0 all-gather.5.cloned.1.call-start
  7.2 0.7 all-gather.5.cloned.1.call-update
  7.9 0.0 all-gather.3.cloned.1.call-start
  7.9 0.7 all-gather.3.cloned.1.call-update
  8.6 0.0 reduce-scatter.5.cloned.1.call-start
  8.7 86.7 %all-gather.5.cloned.1.call-done = bf16[16,32,1024]{2,1,0:T(8,128)(2,1)} async-done(((bf16[1,32,1024]{2,1,0:T(8,128)(2,1)}), bf16[16,32,1024]{2,1,0:T(8,128)(2,1)}) %all-gather.5.cloned.1.call-update) | async-done | bytes 1048592 | tf_op jit(solution)/shard_map/all_gather | solution.py:17
  95.4 86.5 %all-gather.3.cloned.1.call-done = bf16[1024,1024]{1,0:T(8,128)(2,1)} async-done(((bf16[32,1024]{1,0:T(8,128)(2,1)}), bf16[1024,1024]{1,0:T(8,128)(2,1)}) %all-gather.3.cloned.1.call-update) | async-done | bytes 2097168 | tf_op jit(solution)/shard_map/all_gather | solution.py:16
  181.9 3.2 fusion.6
  185.1 34.0 %pmax.15 = f32[512]{0:T(512)S(1)} all-reduce(f32[512]{0:T(512)S(1)} %get-tuple-element.6), channel_id=1, replica_groups=mesh['img'=16,'txt'=32] {'img'}, use_global_device_ids=true, to_apply=%region_6.0 | all-reduce | flops 512 | bytes 4096 | tf_op jit(solution)/shard_map/pmax | solution.py:30
  219.1 84.2 %pmax.14 = f32[1024]{0:T(1024)S(1)} all-reduce(f32[1024]{0:T(1024)S(1)} %get-tuple-element.7), channel_id=1, replica_groups=mesh['img'=16,'txt'=32] {'txt'}, use_global_device_ids=true, to_apply=%region_1.0 | all-reduce | flops 1024 | bytes 8192 | tf_op jit(solution)/shard_map/pmax | solution.py:29
  303.3 2.2 fusion
  305.5 37.5 %psum.22 = f32[512]{0:T(512)S(1)} all-reduce(f32[512]{0:T(512)S(1)} %get-tuple-element.4), channel_id=1, replica_groups=mesh['img'=16,'txt'=32] {'img'}, use_global_device_ids=true, to_apply=%region_8.0 | all-reduce | flops 512 | bytes 4096 | tf_op jit(solution)/shard_map/psum | solution.py:32
  343.0 84.2 %psum.21 = f32[1024]{0:T(1024)S(1)} all-reduce(f32[1024]{0:T(1024)S(1)} %get-tuple-element.5), channel_id=1, replica_groups=mesh['img'=16,'txt'=32] {'txt'}, use_global_device_ids=true, to_apply=%region_3.0 | all-reduce | flops 1024 | bytes 8192 | tf_op jit(solution)/shard_map/psum | solution.py:31
  427.3 0.0 copy-start
  427.3 4.2 convolution_convert_fusion.1
  431.5 0.0 reduce-scatter.5.cloned.1.call-update
  431.5 0.0 reduce-scatter.3.cloned.1.call-start
  431.6 0.0 copy-done
  431.6 3.2 convolution_convert_fusion
  434.8 0.0 reduce-scatter.3.cloned.1.call-update
  434.8 0.7 dynamic-slice_reduce_fusion
  435.5 0.6 dynamic-slice_reduce_fusion.1
  437.9 106.6 %psum.23 = f32[]{:T(128)} all-reduce(f32[]{:T(128)S(6)} %sub.42), channel_id=1, replica_groups=mesh['img'=16,'txt'=32] {'img','txt'}, use_global_device_ids=true, to_apply=%region_11.0 | all-reduce | flops 1 | bytes 8 | tf_op jit(solution)/shard_map/psum | solution.py:41
  545.2 0.0 reduce-scatter.5.cloned.1.call-done
  545.3 100.1 %reduce-scatter.3.cloned.1.call-done = bf16[32,1024]{1,0:T(8,128)(2,1)} async-done(((bf16[1024,1024]{1,0:T(8,128)(2,1)}), bf16[32,1024]{1,0:T(8,128)(2,1)}) %reduce-scatter.3.cloned.1.call-update) | async-done | bytes 65552 | tf_op jit(solution)/shard_map/reduce_scatter | solution.py:51
  (4 shorter events, 0.0 us)
Async XLA Ops:
  7.2 88.2 %all-gather.5.cloned.1.call-start = ((), (), s32[]{:S(2)}) async-start(), calls=%async_computation.3 | async-start | bytes 1114112 | tf_op jit(solution)/shard_map/all_gather | solution.py:17
  7.9 174.0 %all-gather.3.cloned.1.call-start = ((), (), s32[]{:S(2)}) async-start(), calls=%async_computation.2 | async-start | bytes 2162688 | tf_op jit(solution)/shard_map/all_gather | solution.py:16
  8.6 536.6 %reduce-scatter.5.cloned.1.call-start = ((), (), s32[]{:S(2)}) async-start(), calls=%async_computation.5 | async-start | bytes 1114112 | tf_op jit(solution)/shard_map/reduce_scatter | solution.py:54
  427.3 4.3 copy-start
  431.5 213.8 %reduce-scatter.3.cloned.1.call-start = ((), (), s32[]{:S(2)}) async-start(), calls=%async_computation.4 | async-start | bytes 2162688 | tf_op jit(solution)/shard_map/reduce_scatter | solution.py:51
Sparse Core Ops, SparseCore 0:
  10.1 85.2 all-gather.4
  98.5 83.2 all-gather.2
  431.7 83.5 reduce-scatter.4
  520.8 124.5 reduce-scatter.2
where the time goes:
time: 654 us; the launch traced here: 653 us
  blocking collectives  347 us (53%)
  waiting for transfers between devices  275 us (42%)
  between operations  17.4 us (3%)
  matrix products  10.6 us (2%)
    psum x1, blocking collectives, per_device(): contrastive_loss = lax.psum(local_term, ('img', 'txt')) / (2.0 * pair_count)  107 us
    reduce_scatter x1, waiting for transfers between devices, per_device(): lax.psum_scatter(partial_image.astype(jnp.bfloat16), 'txt', scatter_dimen...  100 us
    all_gather x1, waiting for transfers between devices, per_device(): lax.all_gather(texts, 'img', axis=0, tiled=True)  86.7 us
    all_gather x1, waiting for transfers between devices, per_device(): image_block = lax.all_gather(images, 'txt', axis=0, tiled=True)  86.5 us
    psum x1, blocking collectives, per_device(): lax.psum(jnp.sum(jnp.exp(logits - row_peak[:, None]), axis=1), 'txt')  84.2 us
    pmax x1, blocking collectives, per_device(): row_peak = lax.pmax(row_local, 'txt')  84.2 us
    psum x1, blocking collectives, per_device(): lax.psum(jnp.sum(jnp.exp(logits - col_peak[None, :]), axis=0), 'img')  37.5 us
    pmax x1, blocking collectives, per_device(): col_peak = lax.pmax(col_local, 'img')  34 us
  transfers between devices with their start and end apart: 4, of which 3 were waited for; matrix products, arithmetic and copies ran while one was open for 1% of the time, Pallas kernels for 0%

commit v1 on v0

v1 whole, which is shorter than its diff:
```python
import jax
import jax.numpy as jnp
from jax import lax
from jax.experimental import pallas as pl
from jax.experimental.pallas import tpu as pltpu
from jax.sharding import PartitionSpec as P

LOGIT_SCALE = 1.0 / 0.07
MESH = pl.DeviceIdType.MESH
F32 = jnp.float32
BF16 = jnp.bfloat16

N = 4
CORES = 2
ROWS = 32
HALF = ROWS // 2
D = 1024
CHUNK = N * CORES * ROWS
COLS = N * N * ROWS
PAIRS = N * CHUNK * N * N
STRIP = 64


def dma(shape):
    return pltpu.SemaphoreType.DMA(shape)


SCRATCH = dict(
    image=pltpu.VMEM((N, N, CORES, ROWS, D), BF16),
    text=pltpu.VMEM((N, N, ROWS, D), BF16),
    row_exp=pltpu.VMEM((N, CHUNK, COLS), F32),
    col_exp=pltpu.VMEM((N, CHUNK, COLS), F32),
    row_peak=pltpu.VMEM((N, CHUNK, 128), F32),
    row_scale=pltpu.VMEM((N, CHUNK, 128), F32),
    row_log=pltpu.VMEM((CHUNK, 128), F32),
    row_dense=pltpu.VMEM((N, 8, 128), F32),
    col_peak=pltpu.VMEM((N, 8, COLS), F32),
    col_log=pltpu.VMEM((N, 8, COLS), F32),
    diag=pltpu.VMEM((8, 128), F32),
    weights=pltpu.VMEM((N, CHUNK, COLS), BF16),
    part_image=pltpu.VMEM((N, N, CORES, ROWS, D), BF16),
    part_core=pltpu.VMEM((N, N, ROWS, D), BF16),
    xa=pltpu.VMEM((N, N, ROWS, D), BF16),
    xr1=pltpu.VMEM((N, 2, HALF, D), BF16),
    xb=pltpu.VMEM((N, 2, ROWS, D), BF16),
    xr2=pltpu.VMEM((N, 2, ROWS, D), BF16),
    za=pltpu.VMEM((N, ROWS, D), BF16),
    zr1=pltpu.VMEM((2, HALF, D), BF16),
    zb=pltpu.VMEM((2, ROWS, D), BF16),
    zr2=pltpu.VMEM((2, ROWS, D), BF16),
    part_text=pltpu.VMEM((N, N, ROWS, D), BF16),
    yr1=pltpu.VMEM((N, 2, HALF, D), BF16),
    yb=pltpu.VMEM((N, 2, ROWS, D), BF16),
    yr2=pltpu.VMEM((N, 2, ROWS, D), BF16),
    ta=pltpu.VMEM((N, ROWS, D), BF16),
    tr=pltpu.VMEM((N, ROWS, D), BF16),
    row1=pltpu.VMEM((N * CORES, 8, 128), F32),
    row2=pltpu.VMEM((N, 8, 128), F32),
    col1=pltpu.VMEM((N, 8, 128), F32),
    col2=pltpu.VMEM((N, 8, 128), F32),
    loss1=pltpu.VMEM((N * CORES, 8, 128), F32),
    loss2=pltpu.VMEM((N, 8, 128), F32),
    loss3=pltpu.VMEM((N, 8, 128), F32),
    loss4=pltpu.VMEM((N, 8, 128), F32),
    local_sem=dma((2,)),
    gz_s=dma((4,)), gz_r=dma((4,)),
    gx_s=dma((N, 4)), gx_r=dma((N, 4)),
    gc_s=dma((N,)), gc_r=dma((N,)),
    gl_s=dma((N,)), gl_r=dma((N,)),
    gy_s=dma((N, 4)), gy_r=dma((N, 4)),
    r1_s=dma((8,)), r1_r=dma((8,)),
    r2_s=dma((N,)), r2_r=dma((N,)),
    c1_s=dma((N,)), c1_r=dma((N,)),
    c2_s=dma((N,)), c2_r=dma((N,)),
    l1_s=dma((8,)), l1_r=dma((8,)),
    l2_s=dma((N,)), l2_r=dma((N,)),
    l3_s=dma((N,)), l3_r=dma((N,)),
    l4_s=dma((N,)), l4_r=dma((N,)),
    sc_s=dma((N,)), sc_r=dma((N,)),
    sx_s=dma((N, 4)), sx_r=dma((N, 4)),
    sz_s=dma((4,)), sz_r=dma((4,)),
    sy_s=dma((N, 4)), sy_r=dma((N, 4)),
    sl_s=dma((N,)), sl_r=dma((N,)),
)
NAMES = list(SCRATCH)


class Refs:
    def __init__(self, refs):
        for name, ref in zip(NAMES, refs):
            setattr(self, name, ref)


def log_sum(parts):
    peak = parts[0]
    for part in parts[1:]:
        peak = jnp.maximum(peak, part)
    total = jnp.exp(parts[0] - peak)
    for part in parts[1:]:
        total = total + jnp.exp(part - peak)
    return peak + jnp.log(total)


def eye():
    rows = lax.broadcasted_iota(jnp.int32, (128, 128), 0)
    cols = lax.broadcasted_iota(jnp.int32, (128, 128), 1)
    return rows == cols


def kernel(img_hbm, txt_hbm, loss_out, gi_out, gt_out, *refs):
    s = Refs(refs)
    img, txt = lax.axis_index("img"), lax.axis_index("txt")
    y, zl = img // N, lax.rem(img, N)
    zh, xc = txt // (N * CORES), lax.rem(txt, N * CORES)
    x, c = xc // CORES, lax.rem(xc, CORES)

    def up(place, by):
        return lax.rem(place + by, N)

    def at_x(place):
        return (img, (zh * N + place) * CORES + c)

    def at_xc(place):
        return (img, zh * (N * CORES) + place)

    def at_zh(place):
        return (img, place * (N * CORES) + xc)

    def at_y(place):
        return (place * N + zl, txt)

    def at_zl(place):
        return (y * N + place, txt)

    other_core = (img, (zh * N + x) * CORES + (1 - c))

    own_image = pltpu.make_async_copy(img_hbm, s.image.at[zh, x, c], s.local_sem.at[0])
    own_text = pltpu.make_async_copy(txt_hbm.at[0], s.text.at[y, zl], s.local_sem.at[1])
    own_image.start()
    own_text.start()

    barrier = pltpu.get_barrier_semaphore()
    partners = [at_xc(lax.rem(xc + by, N * CORES)) for by in range(1, N * CORES)]
    for by in range(1, N):
        partners += [at_zh(up(zh, by)), at_y(up(y, by)), at_zl(up(zl, by))]
    for partner in partners:
        pl.semaphore_signal(barrier, inc=1, device_id=partner, device_id_type=MESH)
    pl.semaphore_wait(barrier, len(partners))

    sent = []

    def remote(src, dst, send_sem, recv_sem, device):
        return pltpu.make_async_remote_copy(
            src_ref=src, dst_ref=dst, send_sem=send_sem, recv_sem=recv_sem,
            device_id=device, device_id_type=MESH,
        )

    def send(*args):
        copy = remote(*args)
        copy.start()
        sent.append(copy)

    def arrive(dst, send_sem, recv_sem, device):
        remote(dst, dst, send_sem, recv_sem, device).wait_recv()

    low, high = pl.ds(0, HALF), pl.ds(HALF, HALF)

    class Gather:
        def __init__(self, slot, me, device, ss, rs):
            self.slot, self.me, self.device, self.ss, self.rs = slot, me, device, ss, rs
            self.right, self.left, self.far = up(me, 1), up(me, 3), up(me, 2)

        def full(self):
            own = self.slot(self.me)
            send(own, own, self.ss(0), self.rs(0), self.device(self.right))
            send(own, own, self.ss(1), self.rs(1), self.device(self.left))

        def forward_left(self):
            block = self.slot(self.left)
            arrive(block, self.ss(0), self.rs(0), self.device(self.left))
            send(block.at[low], block.at[low], self.ss(2), self.rs(2), self.device(self.right))

        def forward_right(self):
            block = self.slot(self.right)
            arrive(block, self.ss(1), self.rs(1), self.device(self.right))
            send(block.at[high], block.at[high], self.ss(3), self.rs(3), self.device(self.left))

        def forward(self):
            self.forward_left()
            self.forward_right()

        def finish(self):
            block = self.slot(self.far)
            arrive(block.at[low], self.ss(2), self.rs(2), self.device(self.left))
            arrive(block.at[high], self.ss(3), self.rs(3), self.device(self.right))

    class Scatter:
        def __init__(self, slot, r1, b, r2, me, device, ss, rs):
            self.slot, self.r1, self.b, self.r2 = slot, r1, b, r2
            self.me, self.device, self.ss, self.rs = me, device, ss, rs
            self.right, self.left, self.far = up(me, 1), up(me, 3), up(me, 2)

        def first(self):
            block = self.slot(self.far)
            send(block.at[low], self.r1(0), self.ss(0), self.rs(0), self.device(self.right))
            send(block.at[high], self.r1(1), self.ss(1), self.rs(1), self.device(self.left))

        def second(self):
            block, out = self.slot(self.right), self.b(0)
            arrive(self.r1(0), self.ss(0), self.rs(0), self.device(self.left))
            out[low] = (block[low].astype(F32) + self.r1(0)[...].astype(F32)).astype(BF16)
            out[high] = block[high]
            send(out, self.r2(0), self.ss(2), self.rs(2), self.device(self.right))
            block, out = self.slot(self.left), self.b(1)
            arrive(self.r1(1), self.ss(1), self.rs(1), self.device(self.right))
            out[high] = (block[high].astype(F32) + self.r1(1)[...].astype(F32)).astype(BF16)
            out[low] = block[low]
            send(out, self.r2(1), self.ss(3), self.rs(3), self.device(self.left))

        def third(self):
            arrive(self.r2(0), self.ss(2), self.rs(2), self.device(self.left))
            arrive(self.r2(1), self.ss(3), self.rs(3), self.device(self.right))
            total = self.slot(self.me)[...].astype(F32) + self.r2(0)[...].astype(F32)
            return (total + self.r2(1)[...].astype(F32)).astype(BF16)

    def exchange(buf, me, count, device, ss, rs):
        for by in range(1, count):
            peer = lax.rem(me + by, count)
            send(buf.at[me], buf.at[me], ss.at[by], rs.at[by], device(peer))

    def collect(buf, me, count, device, ss, rs):
        for by in range(1, count):
            peer = lax.rem(me + count - by, count)
            arrive(buf.at[peer], ss.at[by], rs.at[by], device(peer))
        return [buf[j] for j in range(count)]

    gz = Gather(lambda o: s.image.at[o, x, c], zh, at_zh, lambda k: s.gz_s.at[k], lambda k: s.gz_r.at[k])
    gx = {
        by: Gather(
            lambda o, zo=up(zh, by): s.image.at[zo, o, c], x, at_x,
            lambda k, zo=up(zh, by): s.gx_s.at[zo, k], lambda k, zo=up(zh, by): s.gx_r.at[zo, k],
        )
        for by in range(N)
    }
    gy = {
        by: Gather(
            lambda o, zo=up(zl, by): s.text.at[o, zo], y, at_y,
            lambda k, zo=up(zl, by): s.gy_s.at[zo, k], lambda k, zo=up(zl, by): s.gy_r.at[zo, k],
        )
        for by in range(N)
    }
    own_image.wait()
    gz.full()
    own_text.wait()
    for by in (1, 3, 2):
        mine = s.text.at[y, zl]
        send(mine, mine, s.gl_s.at[by], s.gl_r.at[by], at_zl(up(zl, by)))
    gx[0].full()
    gy[0].full()
    gz.forward_left()
    gx[3].full()
    gz.forward_right()
    gx[1].full()
    for by in (1, 3, 2):
        peer = up(zl, N - by)
        arrive(s.text.at[y, peer], s.gl_s.at[by], s.gl_r.at[by], at_zl(peer))
        gy[N - by].full()
    gx[0].forward()
    gy[0].forward()
    gx[3].forward()
    gx[1].forward()
    gz.finish()
    gx[2].full()
    for by in (3, 1, 2):
        gy[by].forward()

    def share(by):
        gx[by].finish()
        zo = up(zh, by)
        send(s.image.at[zo, :, c], s.image.at[zo, :, c], s.gc_s.at[zo], s.gc_r.at[zo], other_core)

    share(0)
    share(3)
    share(1)
    for by in (0, 3, 1, 2):
        gy[by].finish()
    gx[2].forward()
    share(2)

    diag_shift = txt * COLS - img * (N * CHUNK)
    col_ids = lax.broadcasted_iota(jnp.int32, (STRIP, COLS), 1) + diag_shift
    row_ids = lax.broadcasted_iota(jnp.int32, (STRIP, COLS), 0)

    def diagonal(zo, first):
        return row_ids + (zo * CHUNK + first) == col_ids

    s.diag[...] = jnp.zeros((8, 128), F32)

    def chunk_stats(k, carry):
        by = jnp.where(k == 1, 3, jnp.where(k == 2, 1, jnp.where(k == 3, 2, 0)))
        zo = lax.rem(zh + by, N)
        arrive(s.image.at[zo, :, 1 - c], s.gc_s.at[zo], s.gc_r.at[zo], other_core)
        s.col_exp[zo] = LOGIT_SCALE * lax.dot_general(
            s.image[zo].reshape(CHUNK, D), s.text[...].reshape(COLS, D),
            (((1,), (1,)), ((), ())), preferred_element_type=F32,
        )
        col_peak = None
        for first in range(0, CHUNK, STRIP):
            rows = slice(first, first + STRIP)
            logits = s.col_exp[zo, rows, :]
            peak = jnp.max(logits, axis=1, keepdims=True)
            exps = jnp.exp(logits - peak)
            s.row_exp[zo, rows, :] = exps
            s.row_peak[zo, rows, :] = jnp.broadcast_to(peak, (STRIP, 128))
            log = peak + jnp.log(jnp.sum(exps, axis=1, keepdims=True))
            s.row_log[rows, :] = jnp.broadcast_to(log, (STRIP, 128))
            part = jnp.max(logits.reshape(STRIP // 8, 8, COLS), axis=0)
            col_peak = part if col_peak is None else jnp.maximum(col_peak, part)
        col_peak = jnp.max(col_peak, axis=0, keepdims=True)
        col_total = jnp.zeros((8, COLS), F32)
        diag = jnp.zeros((8, COLS), F32)
        for first in range(0, CHUNK, STRIP):
            rows = slice(first, first + STRIP)
            logits = s.col_exp[zo, rows, :]
            exps = jnp.exp(logits - col_peak)
            s.col_exp[zo, rows, :] = exps
            col_total = col_total + jnp.sum(exps.reshape(STRIP // 8, 8, COLS), axis=0)
            kept = jnp.where(diagonal(zo, first), logits, 0.0)
            diag = diag + jnp.sum(kept.reshape(STRIP // 8, 8, COLS), axis=0)
        s.diag[...] += diag[:, :128] + diag[:, 128:256] + diag[:, 256:384] + diag[:, 384:]
        s.col_peak[zo] = jnp.broadcast_to(col_peak, (8, COLS))
        col_log = col_peak + jnp.log(jnp.sum(col_total, axis=0, keepdims=True))
        s.col_log[zo] = jnp.broadcast_to(col_log, (8, COLS))
        on = eye()
        top = jnp.sum(jnp.where(on, s.row_log[0:128, :], 0.0), axis=0, keepdims=True)
        low_part = jnp.sum(jnp.where(on, s.row_log[128:256, :], 0.0), axis=0, keepdims=True)
        s.row_dense[zo] = jnp.concatenate([top, low_part] * 4, axis=0)
        return carry

    lax.fori_loop(0, N, chunk_stats, 0)

    s.row1[xc] = jnp.concatenate([s.row_dense[j][0:2] for j in range(N)], axis=0)
    exchange(s.row1, xc, N * CORES, at_xc, s.r1_s, s.r1_r)
    col_local = log_sum([s.col_log[j] for j in range(N)])[0:1]
    dense = [col_local[:, j * 128 : (j + 1) * 128] for j in range(N)]
    s.col1[y] = jnp.concatenate(dense + dense, axis=0)
    exchange(s.col1, y, N, at_y, s.c1_s, s.c1_r)
    s.row2[zh] = log_sum(collect(s.row1, xc, N * CORES, at_xc, s.r1_s, s.r1_r))
    exchange(s.row2, zh, N, at_zh, s.r2_s, s.r2_r)
    s.col2[zl] = log_sum(collect(s.col1, y, N, at_y, s.c1_s, s.c1_r))
    exchange(s.col2, zl, N, at_zl, s.c2_s, s.c2_r)
    row_lse = log_sum(collect(s.row2, zh, N, at_zh, s.r2_s, s.r2_r))
    on = eye()
    for j in range(8):
        spread = jnp.where(on, jnp.broadcast_to(row_lse[j : j + 1], (128, 128)), 0.0)
        column = jnp.sum(spread, axis=1, keepdims=True)
        rows = slice((j % 2) * 128, (j % 2) * 128 + 128)
        s.row_scale[j // 2, rows, :] = (0.5 * LOGIT_SCALE) * jnp.exp(s.row_peak[j // 2, rows, :] - column)
    col_lse = log_sum(collect(s.col2, zl, N, at_zl, s.c2_s, s.c2_r))
    wide_col = jnp.concatenate([col_lse[j : j + 1] for j in range(N)], axis=1)

    def chunk_weights(zo, carry):
        col_scale = (0.5 * LOGIT_SCALE) * jnp.exp(s.col_peak[zo, 0:1, :] - wide_col)
        for first in range(0, CHUNK, STRIP):
            rows = slice(first, first + STRIP)
            row_scale = s.row_scale[zo, rows, :]
            row_scale = jnp.concatenate([row_scale] * (COLS // 128), axis=1)
            value = s.row_exp[zo, rows, :] * row_scale + s.col_exp[zo, rows, :] * col_scale
            value = value - jnp.where(diagonal(zo, first), LOGIT_SCALE, 0.0)
            s.weights[zo, rows, :] = value.astype(BF16)
        return carry

    lax.fori_loop(0, N, chunk_weights, 0)

    share_rows = row_lse * (1.0 / (N * N * CORES))
    share_cols = col_lse * (0.5 / (N * N))
    s.loss1[xc] = share_rows + share_cols - 2.0 * s.diag[...]
    exchange(s.loss1, xc, N * CORES, at_xc, s.l1_s, s.l1_r)

    def grad_text(by):
        place = up(y, by)
        columns = pl.ds(pl.multiple_of(place * (N * ROWS), N * ROWS), N * ROWS)
        w = s.weights[:, :, columns].reshape(N * CHUNK, N * ROWS)
        out = lax.dot_general(
            w, s.image[...].reshape(N * CHUNK, D), (((0,), (0,)), ((), ())), preferred_element_type=F32
        )
        s.part_text[place] = out.astype(BF16).reshape(N, ROWS, D)

    def grad_image(by):
        zo = up(zh, by)
        out = jnp.dot(s.weights[zo], s.text[...].reshape(COLS, D), preferred_element_type=F32)
        s.part_image[zo] = out.astype(BF16).reshape(N, CORES, ROWS, D)
        send(s.part_image.at[zo, :, 1 - c], s.part_core.at[zo], s.sc_s.at[zo], s.sc_r.at[zo], other_core)

    def add_core(by):
        zo = up(zh, by)
        arrive(s.part_core.at[zo], s.sc_s.at[zo], s.sc_r.at[zo], other_core)
        s.xa[zo] = (s.part_image[zo, :, c].astype(F32) + s.part_core[zo].astype(F32)).astype(BF16)

    sx = {
        by: Scatter(
            lambda o, zo=up(zh, by): s.xa.at[zo, o],
            lambda k, zo=up(zh, by): s.xr1.at[zo, k],
            lambda k, zo=up(zh, by): s.xb.at[zo, k],
            lambda k, zo=up(zh, by): s.xr2.at[zo, k],
            x, at_x,
            lambda k, zo=up(zh, by): s.sx_s.at[zo, k],
            lambda k, zo=up(zh, by): s.sx_r.at[zo, k],
        )
        for by in range(N)
    }
    sy = {
        by: Scatter(
            lambda o, zo=up(zl, by): s.part_text.at[o, zo],
            lambda k, zo=up(zl, by): s.yr1.at[zo, k],
            lambda k, zo=up(zl, by): s.yb.at[zo, k],
            lambda k, zo=up(zl, by): s.yr2.at[zo, k],
            y, at_y,
            lambda k, zo=up(zl, by): s.sy_s.at[zo, k],
            lambda k, zo=up(zl, by): s.sy_r.at[zo, k],
        )
        for by in range(N)
    }
    sz = Scatter(
        lambda o: s.za.at[o], lambda k: s.zr1.at[k], lambda k: s.zb.at[k], lambda k: s.zr2.at[k],
        zh, at_zh, lambda k: s.sz_s.at[k], lambda k: s.sz_r.at[k],
    )

    grad_text(2)
    for by in (2, 1, 3, 0):
        sy[by].first()
    grad_image(2)
    grad_text(1)
    grad_text(3)
    add_core(2)
    sx[2].first()
    grad_image(1)
    for by in (2, 1, 3, 0):
        sy[by].second()
    add_core(1)
    sx[1].first()
    grad_image(3)
    sx[2].second()
    add_core(3)
    sx[3].first()
    grad_image(0)
    grad_text(0)
    sx[1].second()
    add_core(0)
    sx[0].first()
    sx[3].second()

    s.za[up(zh, 2)] = sx[2].third()
    sz.first()
    for by in (2, 1, 3):
        peer = up(zl, by)
        s.ta[peer] = sy[by].third()
        send(s.ta.at[peer], s.tr.at[zl], s.sl_s.at[by], s.sl_r.at[by], at_zl(peer))
    sx[0].second()
    s.za[up(zh, 1)] = sx[1].third()
    s.za[up(zh, 3)] = sx[3].third()
    sz.second()

    s.loss2[zh] = sum(collect(s.loss1, xc, N * CORES, at_xc, s.l1_s, s.l1_r))
    exchange(s.loss2, zh, N, at_zh, s.l2_s, s.l2_r)
    text_total = sy[0].third().astype(F32)
    s.loss3[y] = sum(collect(s.loss2, zh, N, at_zh, s.l2_s, s.l2_r))
    exchange(s.loss3, y, N, at_y, s.l3_s, s.l3_r)
    s.za[zh] = sx[0].third()
    s.loss4[zl] = sum(collect(s.loss3, y, N, at_y, s.l3_s, s.l3_r))
    exchange(s.loss4, zl, N, at_zl, s.l4_s, s.l4_r)
    for by in (1, 3, 2):
        peer = up(zl, N - by)
        arrive(s.tr.at[peer], s.sl_s.at[by], s.sl_r.at[by], at_zl(peer))
        text_total = text_total + s.tr[peer].astype(F32)
    gt_out[0] = text_total.astype(BF16)
    gi_out[...] = sz.third()
    total = sum(collect(s.loss4, zl, N, at_zl, s.l4_s, s.l4_r))
    loss_out[0, 0] = jnp.sum(total) / (2.0 * PAIRS)

    for copy in sent:
        copy.wait_send()


def per_device(images, texts):
    loss, grad_images, grad_texts = pl.pallas_call(
        kernel,
        out_shape=(
            jax.ShapeDtypeStruct((1, 1), F32),
            jax.ShapeDtypeStruct((ROWS, D), BF16),
            jax.ShapeDtypeStruct((1, ROWS, D), BF16),
        ),
        in_specs=[pl.BlockSpec(memory_space=pl.ANY)] * 2,
        out_specs=(
            pl.BlockSpec(memory_space=pltpu.SMEM),
            pl.BlockSpec(memory_space=pltpu.VMEM),
            pl.BlockSpec(memory_space=pltpu.VMEM),
        ),
        scratch_shapes=list(SCRATCH.values()),
        compiler_params=pltpu.CompilerParams(
            collective_id=0, has_side_effects=True, vmem_limit_bytes=48 * 1024 * 1024
        ),
        name="contrastive",
    )(images, texts)
    return loss.reshape(()), grad_images, grad_texts


def solution(mesh):
    in_specs = (P(("img", "txt"), None), P("img", "txt", None))
    out_specs = (P(), P(("img", "txt"), None), P("img", "txt", None))
    return jax.shard_map(
        per_device, mesh=mesh, in_specs=in_specs, out_specs=out_specs, check_vma=False
    )
```

time: 654 us -> 100 us (0.15)
  blocking collectives: 347 us -> 0 us
  waiting for transfers between devices: 275 us -> 0 us
  Pallas kernels: 0 us -> 94.5 us
  between operations: 17.4 us -> 2.41 us
  matrix products: 10.6 us -> 0 us
    psum x3 -> x0, blocking collectives: 228 us -> none  [the longest x1 107 us: per_device(): contrastive_loss = lax.psum(local_term, ('img', 'txt')) / (2.0 * pair_count)]
    all_gather x2 -> x0, waiting for transfers between devices: 173 us -> none  [the longest x1 86.7 us: per_device(): lax.all_gather(texts, 'img', axis=0, tiled=True)]
    pmax x2 -> x0, blocking collectives: 118 us -> none  [the longest x1 84.2 us: per_device(): row_peak = lax.pmax(row_local, 'txt')]
    reduce_scatter x2 -> x0, waiting for transfers between devices: 100 us -> none  [the longest x1 100 us: per_device(): lax.psum_scatter(partial_image.astype(jnp.bfloat16), 'txt', scatter_dimen...]
    pallas_call x0 -> x1, Pallas kernels: none -> 94.5 us  [per_device(): pl.pallas_call(kernel, out_shape=(jax.ShapeDtypeStruct((1, 1), F32), jax....]
    dot_general x3 -> x0, matrix products: 10.6 us -> none  [the longest x1 4.22 us: per_device(): lax.dot_general(weights, image_block, (((0,), (0,)), ((), ())), preferred...]
  transfers between devices with their start and end apart: 4 -> 0, of which waited for: 3 -> 0; matrix products, arithmetic and copies ran while one was open for 1% -> 0% of each run, Pallas kernels for 0% -> 0%
where the time goes in v1:
time: 100 us; the launch traced here: 99.8 us
  Pallas kernels  94.5 us (94%)
  local copies, waits for them, and re-layouts  2.93 us (3%)
  between operations  2.41 us (2%)
    pallas_call x1, Pallas kernels, per_device(): pl.pallas_call(kernel, out_shape=(jax.ShapeDtypeStruct((1, 1), F32), jax....  94.5 us
    unnamed x6, local copies, waits for them, and re-layouts  2.93 us

profile of v1, /device:TPU:24, one launch (start us, length us, event | category | flops | bytes accessed | tf_op | source)
XLA Modules:
  0.0 99.8 jit_solution(14803563929032511939)
XLA Ops:
  0.6 0.0 copy-start
  0.6 0.8 copy-done
  1.5 0.0 copy-start.1
  1.5 0.8 copy-done.1
  2.3 94.5 %contrastive.1 = (f32[1,1]{1,0:T(1,128)}, bf16[32,1024]{1,0:T(8,128)(2,1)S(1)}, bf16[1,32,1024]{2,1,0:T(8,128)(2,1)S(1)}) custom-call(bf16[32,1024]{1,0:T(8,128)(2,1)S(1)} %copy-done, bf16[1,32,1024]{2,1,0:T(8,128)(2,1)S(1)} %copy-done.1), custom_call_target="tpu_custom_call" | custom-call | tf_op jit(solution)/shard_map/contrastive/pallas_call | solution.py:486
  97.4 0.6 copy.9
  98.1 0.6 copy.10
Async XLA Ops:
  0.6 0.8 copy-start
  1.5 0.8 copy-start.1

commit v2 on v0

v2 whole, which is shorter than its diff:
```python
import jax
import jax.numpy as jnp
from jax import lax
from jax.experimental import pallas as pl
from jax.experimental.pallas import tpu as pltpu
from jax.sharding import PartitionSpec as P

LOGIT_SCALE = 1.0 / 0.07
MESH = pl.DeviceIdType.MESH
F32 = jnp.float32
BF16 = jnp.bfloat16

N = 4
NZ = 16
CORES = 2
ROWS = 32
D = 1024
WIDE = D // 2
CHUNK = N * ROWS
COLS = N * N * CORES * ROWS
PAIRS = 16384
STRIP = ROWS
FAR = NZ // 2

PIECES = [(pl.ds(0, 16), pl.ds(0, D)), (pl.ds(16, 16), pl.ds(0, D))]
NP = len(PIECES)
UPPER = list(range(NP // 2))
LOWER = list(range(NP // 2, NP))


def dma(*shape):
    return pltpu.SemaphoreType.DMA(shape)


def bf16(*shape):
    return pltpu.VMEM(shape, BF16)


def f32(*shape):
    return pltpu.VMEM(shape, F32)


SCRATCH = dict(
    image=bf16(NZ, ROWS, D),
    text=bf16(N, N, CORES, ROWS, D),
    row_exp=f32(N, CHUNK, COLS),
    col_exp=f32(N, CHUNK, COLS),
    row_peak=f32(N, CHUNK, 128),
    row_scale=f32(N, CHUNK, 128),
    row_log=f32(CHUNK, 128),
    row_dense=f32(N, 8, 128),
    col_peak=f32(N, 8, COLS),
    col_log=f32(N, 8, COLS),
    col_ids=pltpu.VMEM((8, COLS), jnp.int32),
    diag=f32(8, 128),
    weights=bf16(N, CHUNK, COLS),
    part_image=bf16(NZ, ROWS, D),
    z_in=bf16(2, FAR + 1, ROWS, D),
    z_out=bf16(2, FAR + 1, ROWS, D),
    part_text=bf16(N, N, CORES, ROWS, D),
    part_core=bf16(N, N, ROWS, D),
    plane=bf16(N, N, ROWS, D),
    big_in=bf16(2, N, 3, ROWS, WIDE),
    big_out=bf16(2, N, ROWS, WIDE),
    line=bf16(2, N, ROWS, WIDE),
    small_in=bf16(2, 3, ROWS, WIDE),
    small_out=bf16(2, ROWS, WIDE),
    row1=f32(NZ, N, 128),
    col1=f32(N * CORES, 8, 128),
    col2=f32(N, 8, 128),
    loss1=f32(N * CORES, 1, 128),
    loss2=f32(N, 1, 128),
    loss3=f32(NZ, 1, 128),
    local_sem=dma(2),
    zg_s=dma(2, FAR + 1, NP), zg_r=dma(2, FAR + 1, NP),
    small_g_s=dma(2, 3), small_g_r=dma(2, 3),
    big_g_s=dma(2, N, 3), big_g_r=dma(2, N, 3),
    core_g_s=dma(2, N), core_g_r=dma(2, N),
    row1_s=dma(NZ), row1_r=dma(NZ),
    col1_s=dma(N * CORES), col1_r=dma(N * CORES),
    col2_s=dma(N), col2_r=dma(N),
    loss1_s=dma(N * CORES), loss1_r=dma(N * CORES),
    loss2_s=dma(N), loss2_r=dma(N),
    loss3_s=dma(NZ), loss3_r=dma(NZ),
    core_s_s=dma(N), core_s_r=dma(N),
    zs_s=dma(2, FAR + 1, NP), zs_r=dma(2, FAR + 1, NP),
    big_s_s=dma(2, N, 3), big_s_r=dma(2, N, 3),
    small_s_s=dma(2, 3), small_s_r=dma(2, 3),
)
NAMES = list(SCRATCH)


class Refs:
    def __init__(self, refs):
        for name, ref in zip(NAMES, refs):
            setattr(self, name, ref)


def log_sum(parts):
    peak = parts[0]
    for part in parts[1:]:
        peak = jnp.maximum(peak, part)
    total = jnp.exp(parts[0] - peak)
    for part in parts[1:]:
        total = total + jnp.exp(part - peak)
    return peak + jnp.log(total)


def eye():
    rows = lax.broadcasted_iota(jnp.int32, (128, 128), 0)
    cols = lax.broadcasted_iota(jnp.int32, (128, 128), 1)
    return rows == cols


def add(a, b):
    return (a.astype(F32) + b.astype(F32)).astype(BF16)


def kernel(img_hbm, txt_hbm, loss_out, gi_out, gt_out, *refs):
    s = Refs(refs)
    img, txt = lax.axis_index("img"), lax.axis_index("txt")
    y, zl = img // N, lax.rem(img, N)
    zh, xc = txt // (N * CORES), lax.rem(txt, N * CORES)
    x, c = xc // CORES, lax.rem(xc, CORES)
    z = zh * N + zl

    def up(place, by, count=N):
        return lax.rem(place + (by + count) % count, count)

    def at_x(place):
        return (img, (zh * N + place) * CORES + c)

    def at_xc(place):
        return (img, zh * (N * CORES) + place)

    def at_y(place):
        return (place * N + zl, txt)

    def at_z(place):
        return (y * N + lax.rem(place, N), (place // N) * (N * CORES) + xc)

    other_core = (img, (zh * N + x) * CORES + (1 - c))

    own_image = pltpu.make_async_copy(img_hbm, s.image.at[z], s.local_sem.at[0])
    own_text = pltpu.make_async_copy(txt_hbm.at[0], s.text.at[y, x, c], s.local_sem.at[1])
    own_image.start()
    own_text.start()

    barrier = pltpu.get_barrier_semaphore()
    z_right, z_left = at_z(up(z, 1, NZ)), at_z(up(z, -1, NZ))
    partners = [z_right, z_left]
    partners += [at_y(up(y, by)) for by in range(1, N)]
    partners += [at_xc(up(xc, by, N * CORES)) for by in range(1, N * CORES)]
    for partner in partners:
        pl.semaphore_signal(barrier, inc=1, device_id=partner, device_id_type=MESH)
    lane = lax.broadcasted_iota(jnp.int32, (8, COLS), 1)
    s.col_ids[...] = (
        zh * 4096 + lax.rem(lane // 64, 4) * 1024 + lax.rem(lane // 32, 2) * 512
        + (lane // 256) * 128 + zl * 32 + lax.rem(lane, 32)
    )
    pl.semaphore_wait(barrier, len(partners))

    sent = []

    def remote(src, dst, send_sem, recv_sem, device):
        return pltpu.make_async_remote_copy(
            src_ref=src, dst_ref=dst, send_sem=send_sem, recv_sem=recv_sem,
            device_id=device, device_id_type=MESH,
        )

    def send(*args):
        copy = remote(*args)
        copy.start()
        sent.append(copy)

    def arrive(dst, send_sem, recv_sem, device):
        remote(dst, dst, send_sem, recv_sem, device).wait_recv()

    def exchange(buf, me, count, device, ss, rs):
        for by in sorted(range(1, count), key=lambda k: -min(k, count - k)):
            peer = up(me, by, count)
            send(buf.at[me], buf.at[me], ss.at[by], rs.at[by], device(peer))

    def collect(buf, me, count, device, ss, rs):
        for by in sorted(range(1, count), key=lambda k: min(k, count - k)):
            peer = up(me, -by, count)
            arrive(buf.at[peer], ss.at[by], rs.at[by], device(peer))
        return [buf[j] for j in range(count)]

    class Gather:
        def __init__(self, slot, me, device, ss, rs, far_right):
            self.slot, self.me, self.device, self.ss, self.rs = slot, me, device, ss, rs
            self.right, self.left, self.far = up(me, 1), up(me, -1), up(me, 2)
            self.far_right = far_right

        def full(self):
            own = self.slot(self.me)
            pair = [(0, self.right), (1, self.left)]
            for k, to in pair if self.far_right else pair[::-1]:
                send(own, own, self.ss.at[k], self.rs.at[k], self.device(to))

        def forward(self):
            pair = [(0, self.left, self.right), (1, self.right, self.left)]
            for k, origin, to in pair if self.far_right else pair[::-1]:
                block = self.slot(origin)
                arrive(block, self.ss.at[k], self.rs.at[k], self.device(origin))
                if (k == 0) == self.far_right:
                    send(block, block, self.ss.at[2], self.rs.at[2], self.device(to))

        def finish(self):
            origin = self.left if self.far_right else self.right
            arrive(self.slot(self.far), self.ss.at[2], self.rs.at[2], self.device(origin))

    class Scatter:
        def __init__(self, slot, r, b, me, device, ss, rs, far_right):
            self.slot, self.r, self.b = slot, r, b
            self.me, self.device, self.ss, self.rs = me, device, ss, rs
            self.far = up(me, 2)
            self.ahead, self.behind = (up(me, 1), up(me, -1)) if far_right else (up(me, -1), up(me, 1))

        def first(self):
            send(self.slot(self.far), self.r.at[0], self.ss.at[0], self.rs.at[0], self.device(self.ahead))
            send(self.slot(self.behind), self.r.at[1], self.ss.at[1], self.rs.at[1], self.device(self.behind))

        def second(self):
            arrive(self.r.at[0], self.ss.at[0], self.rs.at[0], self.device(self.behind))
            self.b[...] = add(self.slot(self.ahead)[...], self.r[0])
            send(self.b, self.r.at[2], self.ss.at[2], self.rs.at[2], self.device(self.ahead))

        def third(self):
            arrive(self.r.at[1], self.ss.at[1], self.rs.at[1], self.device(self.ahead))
            arrive(self.r.at[2], self.ss.at[2], self.rs.at[2], self.device(self.behind))
            total = self.slot(self.me)[...].astype(F32) + self.r[1].astype(F32)
            return (total + self.r[2].astype(F32)).astype(BF16)

    halves = [pl.ds(0, WIDE), pl.ds(WIDE, WIDE)]
    small_g = [
        Gather(lambda o: s.text.at[y, o, c, :, halves[0]], x, at_x, s.small_g_s.at[0], s.small_g_r.at[0], True),
        Gather(lambda o: s.text.at[o, x, c, :, halves[1]], y, at_y, s.small_g_s.at[1], s.small_g_r.at[1], True),
    ]
    big_g = [
        {
            by: Gather(
                lambda o, q=up(x, by): s.text.at[o, q, c, :, halves[0]], y, at_y,
                s.big_g_s.at[0, up(x, by)], s.big_g_r.at[0, up(x, by)], by % 2 == 0,
            )
            for by in range(N)
        },
        {
            by: Gather(
                lambda o, q=up(y, by): s.text.at[q, o, c, :, halves[1]], x, at_x,
                s.big_g_s.at[1, up(y, by)], s.big_g_r.at[1, up(y, by)], by % 2 == 0,
            )
            for by in range(N)
        },
    ]

    def core_block(h, by, core):
        if h == 0:
            return s.text.at[:, up(x, by), core, :, halves[0]]
        return s.text.at[up(y, by), :, core, :, halves[1]]

    def share(by):
        for h in range(2):
            big_g[h][by].finish()
            q = up(x, by) if h == 0 else up(y, by)
            block = core_block(h, by, c)
            send(block, block, s.core_g_s.at[h, q], s.core_g_r.at[h, q], other_core)

    def z_piece(ref, p):
        return ref.at[PIECES[p][0], PIECES[p][1]]

    def z_own():
        for p in range(NP):
            block = z_piece(s.image.at[z], p)
            send(block, block, s.zg_s.at[0, 1, p], s.zg_r.at[0, 1, p], z_right)
            send(block, block, s.zg_s.at[1, 1, p], s.zg_r.at[1, 1, p], z_left)

    def z_gather(step):
        for p in range(NP):
            for way in range(2):
                if step == FAR and p not in (UPPER, LOWER)[way]:
                    continue
                origin = up(z, -step if way == 0 else step, NZ)
                source, target = (z_left, z_right) if way == 0 else (z_right, z_left)
                block = z_piece(s.image.at[origin], p)
                arrive(block, s.zg_s.at[way, step, p], s.zg_r.at[way, step, p], source)
                if step < FAR - 1 or (step == FAR - 1 and p in (UPPER, LOWER)[way]):
                    send(block, block, s.zg_s.at[way, step + 1, p], s.zg_r.at[way, step + 1, p], target)

    own_image.wait()
    z_own()
    own_text.wait()
    for h in range(2):
        small_g[h].full()
    for h in range(2):
        big_g[h][0].full()
    z_gather(1)
    for h in range(2):
        small_g[h].forward()
        big_g[h][3].full()
        big_g[h][1].full()
    z_gather(2)
    for h in range(2):
        small_g[h].finish()
        big_g[h][2].full()
        big_g[h][0].forward()
    z_gather(3)
    for by in (3, 1):
        for h in range(2):
            big_g[h][by].forward()
    share(0)
    z_gather(4)
    for h in range(2):
        big_g[h][2].forward()
    share(3)
    share(1)
    z_gather(5)
    share(2)
    z_gather(6)
    for by in (0, 3, 1, 2):
        for h in range(2):
            q = up(x, by) if h == 0 else up(y, by)
            arrive(core_block(h, by, 1 - c), s.core_g_s.at[h, q], s.core_g_r.at[h, q], other_core)
    z_gather(7)

    row_place = lax.broadcasted_iota(jnp.int32, (STRIP, COLS), 0)

    def diagonal(q, strip):
        first = y * 4096 + strip * 1024 + (q * N + x) * 64 + c * 32
        return row_place + first == s.col_ids[0:1, :]

    s.diag[...] = jnp.zeros((8, 128), F32)

    def chunk_stats(by):
        q = lax.rem(zh + by, N)
        images = s.image[pl.ds(q * N, N)].reshape(CHUNK, D)
        s.col_exp[q] = LOGIT_SCALE * lax.dot_general(
            images, s.text[...].reshape(COLS, D), (((1,), (1,)), ((), ())), preferred_element_type=F32
        )
        col_peak = None
        for strip in range(N):
            rows = slice(strip * STRIP, (strip + 1) * STRIP)
            logits = s.col_exp[q, rows, :]
            peak = jnp.max(logits, axis=1, keepdims=True)
            exps = jnp.exp(logits - peak)
            s.row_exp[q, rows, :] = exps
            s.row_peak[q, rows, :] = jnp.broadcast_to(peak, (STRIP, 128))
            log = peak + jnp.log(jnp.sum(exps, axis=1, keepdims=True))
            s.row_log[rows, :] = jnp.broadcast_to(log, (STRIP, 128))
            part = jnp.max(logits.reshape(STRIP // 8, 8, COLS), axis=0)
            col_peak = part if col_peak is None else jnp.maximum(col_peak, part)
        col_peak = jnp.max(col_peak, axis=0, keepdims=True)
        col_total = jnp.zeros((8, COLS), F32)
        diag = jnp.zeros((8, COLS), F32)
        for strip in range(N):
            rows = slice(strip * STRIP, (strip + 1) * STRIP)
            logits = s.col_exp[q, rows, :]
            exps = jnp.exp(logits - col_peak)
            s.col_exp[q, rows, :] = exps
            col_total = col_total + jnp.sum(exps.reshape(STRIP // 8, 8, COLS), axis=0)
            kept = jnp.where(diagonal(q, strip), logits, 0.0)
            diag = diag + jnp.sum(kept.reshape(STRIP // 8, 8, COLS), axis=0)
        s.diag[...] += sum(diag[:, j * 128 : (j + 1) * 128] for j in range(COLS // 128))
        s.col_peak[q] = jnp.broadcast_to(col_peak, (8, COLS))
        col_log = col_peak + jnp.log(jnp.sum(col_total, axis=0, keepdims=True))
        s.col_log[q] = jnp.broadcast_to(col_log, (8, COLS))
        dense = jnp.sum(jnp.where(eye(), s.row_log[...], 0.0), axis=0, keepdims=True)
        s.row_dense[q] = jnp.broadcast_to(dense, (8, 128))

    def near_chunk(k, carry):
        chunk_stats(jnp.where(k == 2, 3, k))
        return carry

    lax.fori_loop(0, 3, near_chunk, 0)
    z_gather(8)
    chunk_stats(2)

    s.row1[z] = jnp.concatenate([s.row_dense[j][0:1] for j in range(N)], axis=0)
    exchange(s.row1, z, NZ, at_z, s.row1_s, s.row1_r)
    col_local = log_sum([s.col_log[j] for j in range(N)])[0:1]
    s.col1[xc] = jnp.concatenate([col_local[:, j * 128 : (j + 1) * 128] for j in range(8)], axis=0)
    exchange(s.col1, xc, N * CORES, at_xc, s.col1_s, s.col1_r)
    s.col2[y] = log_sum(collect(s.col1, xc, N * CORES, at_xc, s.col1_s, s.col1_r))
    exchange(s.col2, y, N, at_y, s.col2_s, s.col2_r)
    col_lse = log_sum(collect(s.col2, y, N, at_y, s.col2_s, s.col2_r))
    wide_col = jnp.concatenate([col_lse[j : j + 1] for j in range(8)], axis=1)
    row_lse = log_sum(collect(s.row1, z, NZ, at_z, s.row1_s, s.row1_r))
    on = eye()
    for j in range(N):
        spread = jnp.where(on, jnp.broadcast_to(row_lse[j : j + 1], (128, 128)), 0.0)
        column = jnp.sum(spread, axis=1, keepdims=True)
        s.row_scale[j] = (0.5 * LOGIT_SCALE) * jnp.exp(s.row_peak[j] - column)

    def chunk_weights(q, carry):
        col_scale = (0.5 * LOGIT_SCALE) * jnp.exp(s.col_peak[q, 0:1, :] - wide_col)
        for strip in range(N):
            rows = slice(strip * STRIP, (strip + 1) * STRIP)
            row_scale = jnp.concatenate([s.row_scale[q, rows, :]] * (COLS // 128), axis=1)
            value = s.row_exp[q, rows, :] * row_scale + s.col_exp[q, rows, :] * col_scale
            value = value - jnp.where(diagonal(q, strip), LOGIT_SCALE, 0.0)
            s.weights[q, rows, :] = value.astype(BF16)
        return carry

    lax.fori_loop(0, N, chunk_weights, 0)

    def grad_image(by):
        q = up(zh, by)
        out = jnp.dot(s.weights[q], s.text[...].reshape(COLS, D), preferred_element_type=F32)
        s.part_image[pl.ds(q * N, N)] = out.astype(BF16).reshape(N, ROWS, D)

    def z_scatter(step):
        for p in range(NP):
            for way in range(2):
                mine = p in (UPPER, LOWER)[way]
                if step == 1 and not mine:
                    continue
                by = FAR + 1 - step
                block = z_piece(s.part_image.at[up(z, by if way == 0 else -by, NZ)], p)
                source, target = (z_left, z_right) if way == 0 else (z_right, z_left)
                if step > 2 or (step == 2 and mine):
                    got = z_piece(s.z_in.at[way, step - 1], p)
                    arrive(got, s.zs_s.at[way, step - 1, p], s.zs_r.at[way, step - 1, p], source)
                    out = z_piece(s.z_out.at[way, step], p)
                    out[...] = add(block[...], got[...])
                    block = out
                there = z_piece(s.z_in.at[way, step], p)
                send(block, there, s.zs_s.at[way, step, p], s.zs_r.at[way, step, p], target)

    def z_last():
        for p in range(NP):
            total = z_piece(s.part_image.at[z], p)[...].astype(F32)
            for way in range(2):
                got = z_piece(s.z_in.at[way, FAR], p)
                source = (z_left, z_right)[way]
                arrive(got, s.zs_s.at[way, FAR, p], s.zs_r.at[way, FAR, p], source)
                total = total + got[...].astype(F32)
            gi_out[PIECES[p][0], PIECES[p][1]] = total.astype(BF16)

    def grad_text(by):
        place = up(y, by)
        wide = N * CORES * ROWS
        columns = pl.ds(pl.multiple_of(place * wide, wide), wide)
        w = s.weights[:, :, columns].reshape(N * CHUNK, wide)
        out = lax.dot_general(
            w, s.image[...].reshape(NZ * ROWS, D), (((0,), (0,)), ((), ())), preferred_element_type=F32
        )
        s.part_text[place] = out.astype(BF16).reshape(N, CORES, ROWS, D)
        send(s.part_text.at[place, :, 1 - c], s.part_core.at[place], s.core_s_s.at[by], s.core_s_r.at[by], other_core)

    def add_core(by):
        place = up(y, by)
        arrive(s.part_core.at[place], s.core_s_s.at[by], s.core_s_r.at[by], other_core)
        s.plane[place] = add(s.part_text[place, :, c], s.part_core[place])

    big_s = [
        {
            by: Scatter(
                lambda o, q=up(x, by): s.plane.at[o, q, :, halves[0]],
                s.big_in.at[0, up(x, by)], s.big_out.at[0, up(x, by)], y, at_y,
                s.big_s_s.at[0, up(x, by)], s.big_s_r.at[0, up(x, by)], by % 2 == 0,
            )
            for by in range(N)
        },
        {
            by: Scatter(
                lambda o, q=up(y, by): s.plane.at[q, o, :, halves[1]],
                s.big_in.at[1, up(y, by)], s.big_out.at[1, up(y, by)], x, at_x,
                s.big_s_s.at[1, up(y, by)], s.big_s_r.at[1, up(y, by)], by % 2 == 0,
            )
            for by in range(N)
        },
    ]
    small_s = [
        Scatter(
            lambda o: s.line.at[0, o], s.small_in.at[0], s.small_out.at[0], x, at_x,
            s.small_s_s.at[0], s.small_s_r.at[0], True,
        ),
        Scatter(
            lambda o: s.line.at[1, o], s.small_in.at[1], s.small_out.at[1], y, at_y,
            s.small_s_s.at[1], s.small_s_r.at[1], True,
        ),
    ]

    def fold(by):
        for h in range(2):
            q = up(x, by) if h == 0 else up(y, by)
            s.line[h, q] = big_s[h][by].third()

    grad_image(2)
    z_scatter(1)
    grad_image(1)
    grad_image(3)
    z_scatter(2)
    grad_image(0)
    for by in (2, 1, 3, 0):
        grad_text(by)
    z_scatter(3)

    share_rows = jnp.sum(row_lse) * (1.0 / NZ)
    share_cols = jnp.sum(col_lse) * (1.0 / (N * N * CORES))
    own_share = share_rows + share_cols - 2.0 * jnp.sum(s.diag[...])
    s.loss1[xc] = jnp.full((1, 128), own_share, F32)
    exchange(s.loss1, xc, N * CORES, at_xc, s.loss1_s, s.loss1_r)

    for by in (2, 1, 3, 0):
        add_core(by)
        big_s[1][by].first()
    for by in (2, 1, 3, 0):
        big_s[0][by].first()
    z_scatter(4)
    for by in (2, 1):
        big_s[1][by].second()
    z_scatter(5)
    for by in (3, 0):
        big_s[1][by].second()
    s.loss2[y] = sum(collect(s.loss1, xc, N * CORES, at_xc, s.loss1_s, s.loss1_r))
    exchange(s.loss2, y, N, at_y, s.loss2_s, s.loss2_r)
    for by in (2, 1, 3, 0):
        big_s[0][by].second()
    z_scatter(6)
    fold(2)
    fold(1)
    fold(3)
    s.loss3[z] = sum(collect(s.loss2, y, N, at_y, s.loss2_s, s.loss2_r))
    exchange(s.loss3, z, NZ, at_z, s.loss3_s, s.loss3_r)
    z_scatter(7)
    for h in range(2):
        small_s[h].first()
    fold(0)
    z_scatter(8)
    for h in range(2):
        small_s[h].second()
    for h in range(2):
        gt_out[0, :, halves[h]] = small_s[h].third()
    total = sum(collect(s.loss3, z, NZ, at_z, s.loss3_s, s.loss3_r))
    loss_out[0, 0] = jnp.max(total) / (2.0 * PAIRS)
    z_last()

    for copy in sent:
        copy.wait_send()


def per_device(images, texts):
    loss, grad_images, grad_texts = pl.pallas_call(
        kernel,
        out_shape=(
            jax.ShapeDtypeStruct((1, 1), F32),
            jax.ShapeDtypeStruct((ROWS, D), BF16),
            jax.ShapeDtypeStruct((1, ROWS, D), BF16),
        ),
        in_specs=[pl.BlockSpec(memory_space=pl.ANY)] * 2,
        out_specs=(
            pl.BlockSpec(memory_space=pltpu.SMEM),
            pl.BlockSpec(memory_space=pltpu.VMEM),
            pl.BlockSpec(memory_space=pltpu.VMEM),
        ),
        scratch_shapes=list(SCRATCH.values()),
        compiler_params=pltpu.CompilerParams(
            collective_id=0, has_side_effects=True, vmem_limit_bytes=48 * 1024 * 1024
        ),
        name="contrastive",
    )(images, texts)
    return loss.reshape(()), grad_images, grad_texts


def solution(mesh):
    in_specs = (P(("img", "txt"), None), P("img", "txt", None))
    out_specs = (P(), P(("img", "txt"), None), P("img", "txt", None))
    return jax.shard_map(
        per_device, mesh=mesh, in_specs=in_specs, out_specs=out_specs, check_vma=False
    )
```

time: 654 us -> 86.9 us (0.13)
  blocking collectives: 347 us -> 0 us
  waiting for transfers between devices: 275 us -> 0 us
  Pallas kernels: 0 us -> 80.1 us
  between operations: 17.4 us -> 2.41 us
  matrix products: 10.6 us -> 0 us
    psum x3 -> x0, blocking collectives: 228 us -> none  [the longest x1 107 us: per_device(): contrastive_loss = lax.psum(local_term, ('img', 'txt')) / (2.0 * pair_count)]
    all_gather x2 -> x0, waiting for transfers between devices: 173 us -> none  [the longest x1 86.7 us: per_device(): lax.all_gather(texts, 'img', axis=0, tiled=True)]
    pmax x2 -> x0, blocking collectives: 118 us -> none  [the longest x1 84.2 us: per_device(): row_peak = lax.pmax(row_local, 'txt')]
    reduce_scatter x2 -> x0, waiting for transfers between devices: 100 us -> none  [the longest x1 100 us: per_device(): lax.psum_scatter(partial_image.astype(jnp.bfloat16), 'txt', scatter_dimen...]
    pallas_call x0 -> x1, Pallas kernels: none -> 80.1 us  [per_device(): pl.pallas_call(kernel, out_shape=(jax.ShapeDtypeStruct((1, 1), F32), jax....]
    dot_general x3 -> x0, matrix products: 10.6 us -> none  [the longest x1 4.22 us: per_device(): lax.dot_general(weights, image_block, (((0,), (0,)), ((), ())), preferred...]
  transfers between devices with their start and end apart: 4 -> 0, of which waited for: 3 -> 0; matrix products, arithmetic and copies ran while one was open for 1% -> 0% of each run, Pallas kernels for 0% -> 0%
where the time goes in v2:
time: 86.9 us; the launch traced here: 85.5 us
  Pallas kernels  80.1 us (92%)
  local copies, waits for them, and re-layouts  2.93 us (3%)
  between operations  2.41 us (3%)
    pallas_call x1, Pallas kernels, per_device(): pl.pallas_call(kernel, out_shape=(jax.ShapeDtypeStruct((1, 1), F32), jax....  80.1 us
    unnamed x6, local copies, waits for them, and re-layouts  2.93 us

profile of v2, /device:TPU:24, one launch (start us, length us, event | category | flops | bytes accessed | tf_op | source)
XLA Modules:
  0.0 85.5 jit_solution(1622923821711920813)
XLA Ops:
  0.6 0.0 copy-start
  0.6 0.8 copy-done
  1.5 0.0 copy-start.1
  1.5 0.8 copy-done.1
  2.3 80.1 %contrastive.1 = (f32[1,1]{1,0:T(1,128)}, bf16[32,1024]{1,0:T(8,128)(2,1)S(1)}, bf16[1,32,1024]{2,1,0:T(8,128)(2,1)S(1)}) custom-call(bf16[32,1024]{1,0:T(8,128)(2,1)S(1)} %copy-done, bf16[1,32,1024]{2,1,0:T(8,128)(2,1)S(1)} %copy-done.1), custom_call_target="tpu_custom_call" | custom-call | tf_op jit(solution)/shard_map/contrastive/pallas_call | solution.py:545
  83.1 0.6 copy.9
  83.7 0.6 copy.10
Async XLA Ops:
  0.6 0.8 copy-start
  1.5 0.8 copy-start.1

commit v3 on v2

--- a/solution.py
+++ b/solution.py
@@ -21,12 +21,6 @@
 PAIRS = 16384
 STRIP = ROWS
 FAR = NZ // 2
-
-PIECES = [(pl.ds(0, 16), pl.ds(0, D)), (pl.ds(16, 16), pl.ds(0, D))]
-NP = len(PIECES)
-UPPER = list(range(NP // 2))
-LOWER = list(range(NP // 2, NP))
-
 
 def dma(*shape):
     return pltpu.SemaphoreType.DMA(shape)
@@ -56,15 +50,13 @@
     weights=bf16(N, CHUNK, COLS),
     part_image=bf16(NZ, ROWS, D),
     z_in=bf16(2, FAR + 1, ROWS, D),
-    z_out=bf16(2, FAR + 1, ROWS, D),
+    z_out=bf16(2, 2, ROWS, D),
     part_text=bf16(N, N, CORES, ROWS, D),
     part_core=bf16(N, N, ROWS, D),
     plane=bf16(N, N, ROWS, D),
-    big_in=bf16(2, N, 3, ROWS, WIDE),
-    big_out=bf16(2, N, ROWS, WIDE),
+    big_in=bf16(2, N, N, ROWS, WIDE),
     line=bf16(2, N, ROWS, WIDE),
-    small_in=bf16(2, 3, ROWS, WIDE),
-    small_out=bf16(2, ROWS, WIDE),
+    small_in=bf16(2, N, ROWS, WIDE),
     row1=f32(NZ, N, 128),
     col1=f32(N * CORES, 8, 128),
     col2=f32(N, 8, 128),
@@ -72,9 +64,9 @@
     loss2=f32(N, 1, 128),
     loss3=f32(NZ, 1, 128),
     local_sem=dma(2),
-    zg_s=dma(2, FAR + 1, NP), zg_r=dma(2, FAR + 1, NP),
-    small_g_s=dma(2, 3), small_g_r=dma(2, 3),
-    big_g_s=dma(2, N, 3), big_g_r=dma(2, N, 3),
+    zg_s=dma(2, FAR + 1), zg_r=dma(2, FAR + 1),
+    small_g_s=dma(2, N), small_g_r=dma(2, N),
+    big_g_s=dma(2, N, N), big_g_r=dma(2, N, N),
     core_g_s=dma(2, N), core_g_r=dma(2, N),
     row1_s=dma(NZ), row1_r=dma(NZ),
     col1_s=dma(N * CORES), col1_r=dma(N * CORES),
@@ -83,9 +75,9 @@
     loss2_s=dma(N), loss2_r=dma(N),
     loss3_s=dma(NZ), loss3_r=dma(NZ),
     core_s_s=dma(N), core_s_r=dma(N),
-    zs_s=dma(2, FAR + 1, NP), zs_r=dma(2, FAR + 1, NP),
-    big_s_s=dma(2, N, 3), big_s_r=dma(2, N, 3),
-    small_s_s=dma(2, 3), small_s_r=dma(2, 3),
+    zs_s=dma(2, FAR + 1), zs_r=dma(2, FAR + 1),
+    big_s_s=dma(2, N, N), big_s_r=dma(2, N, N),
+    small_s_s=dma(2, N), small_s_r=dma(2, N),
 )
 NAMES = list(SCRATCH)
 
@@ -147,10 +139,9 @@
     own_text.start()
 
     barrier = pltpu.get_barrier_semaphore()
-    z_right, z_left = at_z(up(z, 1, NZ)), at_z(up(z, -1, NZ))
-    partners = [z_right, z_left]
-    partners += [at_y(up(y, by)) for by in range(1, N)]
-    partners += [at_xc(up(xc, by, N * CORES)) for by in range(1, N * CORES)]
+    partners = [at_z(up(z, by, NZ)) for by in (3, -3, 2, -2, 1, -1)]
+    partners += [at_y(up(y, by)) for by in range(1, N)] + [at_x(up(x, by)) for by in range(1, N)]
+    partners += [other_core]
     for partner in partners:
         pl.semaphore_signal(barrier, inc=1, device_id=partner, device_id_type=MESH)
     lane = lax.broadcasted_iota(jnp.int32, (8, COLS), 1)
@@ -188,71 +179,74 @@
         return [buf[j] for j in range(count)]
 
     class Gather:
-        def __init__(self, slot, me, device, ss, rs, far_right):
+        def __init__(self, slot, me, device, ss, rs):
             self.slot, self.me, self.device, self.ss, self.rs = slot, me, device, ss, rs
-            self.right, self.left, self.far = up(me, 1), up(me, -1), up(me, 2)
-            self.far_right = far_right
-
-        def full(self):
+
+        def start(self):
             own = self.slot(self.me)
-            pair = [(0, self.right), (1, self.left)]
-            for k, to in pair if self.far_right else pair[::-1]:
-                send(own, own, self.ss.at[k], self.rs.at[k], self.device(to))
-
-        def forward(self):
-            pair = [(0, self.left, self.right), (1, self.right, self.left)]
-            for k, origin, to in pair if self.far_right else pair[::-1]:
-                block = self.slot(origin)
-                arrive(block, self.ss.at[k], self.rs.at[k], self.device(origin))
-                if (k == 0) == self.far_right:
-                    send(block, block, self.ss.at[2], self.rs.at[2], self.device(to))
+            for by in (2, 1, 3):
+                send(own, own, self.ss.at[by], self.rs.at[by], self.device(up(self.me, by)))
+
+        def wait(self, by):
+            origin = up(self.me, by)
+            arrive(self.slot(origin), self.ss.at[N - by], self.rs.at[N - by], self.device(origin))
+
+    class Scatter:
+        def __init__(self, slot, r, me, device, ss, rs):
+            self.slot, self.r = slot, r
+            self.me, self.device, self.ss, self.rs = me, device, ss, rs
+
+        def start(self):
+            for by in (2, 1, 3):
+                to = up(self.me, by)
+                send(self.slot(to), self.r.at[by], self.ss.at[by], self.rs.at[by], self.device(to))
 
         def finish(self):
-            origin = self.left if self.far_right else self.right
-            arrive(self.slot(self.far), self.ss.at[2], self.rs.at[2], self.device(origin))
-
-    class Scatter:
-        def __init__(self, slot, r, b, me, device, ss, rs, far_right):
-            self.slot, self.r, self.b = slot, r, b
-            self.me, self.device, self.ss, self.rs = me, device, ss, rs
-            self.far = up(me, 2)
-            self.ahead, self.behind = (up(me, 1), up(me, -1)) if far_right else (up(me, -1), up(me, 1))
-
-        def first(self):
-            send(self.slot(self.far), self.r.at[0], self.ss.at[0], self.rs.at[0], self.device(self.ahead))
-            send(self.slot(self.behind), self.r.at[1], self.ss.at[1], self.rs.at[1], self.device(self.behind))
-
-        def second(self):
-            arrive(self.r.at[0], self.ss.at[0], self.rs.at[0], self.device(self.behind))
-            self.b[...] = add(self.slot(self.ahead)[...], self.r[0])
-            send(self.b, self.r.at[2], self.ss.at[2], self.rs.at[2], self.device(self.ahead))
-
-        def third(self):
-            arrive(self.r.at[1], self.ss.at[1], self.rs.at[1], self.device(self.ahead))
-            arrive(self.r.at[2], self.ss.at[2], self.rs.at[2], self.device(self.behind))
-            total = self.slot(self.me)[...].astype(F32) + self.r[1].astype(F32)
-            return (total + self.r[2].astype(F32)).astype(BF16)
+            total = self.slot(self.me)[...].astype(F32)
+            for by in (1, 3, 2):
+                arrive(self.r.at[by], self.ss.at[by], self.rs.at[by], self.device(up(self.me, -by)))
+                total = total + self.r[by].astype(F32)
+            return total.astype(BF16)
+
+    upper, lower = pl.ds(0, ROWS // 2), pl.ds(ROWS // 2, ROWS // 2)
+    ends = (upper, lower)
+
+    def along(way, steps):
+        return at_z(up(z, steps if way == 0 else -steps, NZ))
+
+    def z_block(way, steps):
+        block = s.image.at[up(z, -steps if way == 0 else steps, NZ)]
+        return block.at[ends[way]] if steps == FAR else block
+
+    def z_send(way, held, reach):
+        block = s.image.at[up(z, -held if way == 0 else held, NZ)]
+        if reach == FAR:
+            block = block.at[ends[way]]
+        send(block, block, s.zg_s.at[way, reach], s.zg_r.at[way, reach], along(way, reach - held))
+
+    def z_wait(way, steps):
+        arrive(z_block(way, steps), s.zg_s.at[way, steps], s.zg_r.at[way, steps], along(way, -1))
 
     halves = [pl.ds(0, WIDE), pl.ds(WIDE, WIDE)]
     small_g = [
-        Gather(lambda o: s.text.at[y, o, c, :, halves[0]], x, at_x, s.small_g_s.at[0], s.small_g_r.at[0], True),
-        Gather(lambda o: s.text.at[o, x, c, :, halves[1]], y, at_y, s.small_g_s.at[1], s.small_g_r.at[1], True),
+        Gather(lambda o: s.text.at[y, o, c, :, halves[0]], x, at_x, s.small_g_s.at[0], s.small_g_r.at[0]),
+        Gather(lambda o: s.text.at[o, x, c, :, halves[1]], y, at_y, s.small_g_s.at[1], s.small_g_r.at[1]),
     ]
     big_g = [
-        {
-            by: Gather(
+        [
+            Gather(
                 lambda o, q=up(x, by): s.text.at[o, q, c, :, halves[0]], y, at_y,
-                s.big_g_s.at[0, up(x, by)], s.big_g_r.at[0, up(x, by)], by % 2 == 0,
+                s.big_g_s.at[0, up(x, by)], s.big_g_r.at[0, up(x, by)],
             )
             for by in range(N)
-        },
-        {
-            by: Gather(
+        ],
+        [
+            Gather(
                 lambda o, q=up(y, by): s.text.at[q, o, c, :, halves[1]], x, at_x,
-                s.big_g_s.at[1, up(y, by)], s.big_g_r.at[1, up(y, by)], by % 2 == 0,
+                s.big_g_s.at[1, up(y, by)], s.big_g_r.at[1, up(y, by)],
             )
             for by in range(N)
-        },
+        ],
     ]
 
     def core_block(h, by, core):
@@ -262,67 +256,44 @@
 
     def share(by):
         for h in range(2):
-            big_g[h][by].finish()
+            for other in (1, 3, 2):
+                big_g[h][by].wait(other)
             q = up(x, by) if h == 0 else up(y, by)
             block = core_block(h, by, c)
             send(block, block, s.core_g_s.at[h, q], s.core_g_r.at[h, q], other_core)
 
-    def z_piece(ref, p):
-        return ref.at[PIECES[p][0], PIECES[p][1]]
-
-    def z_own():
-        for p in range(NP):
-            block = z_piece(s.image.at[z], p)
-            send(block, block, s.zg_s.at[0, 1, p], s.zg_r.at[0, 1, p], z_right)
-            send(block, block, s.zg_s.at[1, 1, p], s.zg_r.at[1, 1, p], z_left)
-
-    def z_gather(step):
-        for p in range(NP):
-            for way in range(2):
-                if step == FAR and p not in (UPPER, LOWER)[way]:
-                    continue
-                origin = up(z, -step if way == 0 else step, NZ)
-                source, target = (z_left, z_right) if way == 0 else (z_right, z_left)
-                block = z_piece(s.image.at[origin], p)
-                arrive(block, s.zg_s.at[way, step, p], s.zg_r.at[way, step, p], source)
-                if step < FAR - 1 or (step == FAR - 1 and p in (UPPER, LOWER)[way]):
-                    send(block, block, s.zg_s.at[way, step + 1, p], s.zg_r.at[way, step + 1, p], target)
-
     own_image.wait()
-    z_own()
+    for reach in (3, 1):
+        for way in range(2):
+            z_send(way, 0, reach)
     own_text.wait()
     for h in range(2):
-        small_g[h].full()
+        small_g[h].start()
     for h in range(2):
-        big_g[h][0].full()
-    z_gather(1)
-    for h in range(2):
-        small_g[h].forward()
-        big_g[h][3].full()
-        big_g[h][1].full()
-    z_gather(2)
-    for h in range(2):
-        small_g[h].finish()
-        big_g[h][2].full()
-        big_g[h][0].forward()
-    z_gather(3)
-    for by in (3, 1):
+        big_g[h][0].start()
+    for by in (1, 3, 2):
         for h in range(2):
-            big_g[h][by].forward()
+            small_g[h].wait(by)
+            big_g[h][by].start()
+    for way in range(2):
+        z_wait(way, 3)
+        for reach in (6, 4, 2):
+            z_send(way, 3, reach)
     share(0)
-    z_gather(4)
-    for h in range(2):
-        big_g[h][2].forward()
+    share(1)
+    for way in range(2):
+        z_wait(way, 6)
+        for reach in (8, 7, 5):
+            z_send(way, 6, reach)
     share(3)
-    share(1)
-    z_gather(5)
     share(2)
-    z_gather(6)
-    for by in (0, 3, 1, 2):
+    for by in (0, 1, 3, 2):
         for h in range(2):
             q = up(x, by) if h == 0 else up(y, by)
             arrive(core_block(h, by, 1 - c), s.core_g_s.at[h, q], s.core_g_r.at[h, q], other_core)
-    z_gather(7)
+    for steps in (1, 2):
+        for way in range(2):
+            z_wait(way, steps)
 
     row_place = lax.broadcasted_iota(jnp.int32, (STRIP, COLS), 0)
 
@@ -368,12 +339,18 @@
         dense = jnp.sum(jnp.where(eye(), s.row_log[...], 0.0), axis=0, keepdims=True)
         s.row_dense[q] = jnp.broadcast_to(dense, (8, 128))
 
+    chunk_stats(0)
+    for steps in (4, 5, 7):
+        for way in range(2):
+            z_wait(way, steps)
+
     def near_chunk(k, carry):
-        chunk_stats(jnp.where(k == 2, 3, k))
+        chunk_stats(1 + 2 * k)
         return carry
 
-    lax.fori_loop(0, 3, near_chunk, 0)
-    z_gather(8)
+    lax.fori_loop(0, 2, near_chunk, 0)
+    for way in range(2):
+        z_wait(way, FAR)
     chunk_stats(2)
 
     s.row1[z] = jnp.concatenate([s.row_dense[j][0:1] for j in range(N)], axis=0)
@@ -409,33 +386,42 @@
         out = jnp.dot(s.weights[q], s.text[...].reshape(COLS, D), preferred_element_type=F32)
         s.part_image[pl.ds(q * N, N)] = out.astype(BF16).reshape(N, ROWS, D)
 
-    def z_scatter(step):
-        for p in range(NP):
+    def z_part(way, steps):
+        return s.part_image.at[up(z, -steps if way == 0 else steps, NZ)]
+
+    def z_give(steps, target):
+        for way in range(2):
+            block, there = z_part(way, steps), s.z_in.at[way, steps]
+            if steps == FAR:
+                block, there = block.at[ends[way]], there.at[ends[way]]
+            send(block, there, s.zs_s.at[way, steps], s.zs_r.at[way, steps], along(way, -target))
+
+    def z_take(way, steps):
+        got = s.z_in.at[way, steps]
+        if steps == FAR:
+            got = got.at[ends[way]]
+        arrive(got, s.zs_s.at[way, steps], s.zs_r.at[way, steps], along(way, 1))
+
+    def z_hub(way, steps, parts):
+        total = z_part(way, steps)[...].astype(F32)
+        for part in parts:
+            z_take(way, part)
+        for part in parts:
+            if part != FAR:
+                total = total + s.z_in[way, part].astype(F32)
+        out = s.z_out.at[way, steps // 3 - 1]
+        out[...] = total.astype(BF16)
+        if FAR in parts:
+            out[ends[way]] = (total[ends[way].start : ends[way].start + ends[way].size] + s.z_in[way, FAR, ends[way]].astype(F32)).astype(BF16)
+        send(out, s.z_in.at[way, steps], s.zs_s.at[way, steps], s.zs_r.at[way, steps], along(way, -3))
+
+    def z_last():
+        total = s.part_image[z].astype(F32)
+        for steps in (1, 3):
             for way in range(2):
-                mine = p in (UPPER, LOWER)[way]
-                if step == 1 and not mine:
-                    continue
-                by = FAR + 1 - step
-                block = z_piece(s.part_image.at[up(z, by if way == 0 else -by, NZ)], p)
-                source, target = (z_left, z_right) if way == 0 else (z_right, z_left)
-                if step > 2 or (step == 2 and mine):
-                    got = z_piece(s.z_in.at[way, step - 1], p)
-                    arrive(got, s.zs_s.at[way, step - 1, p], s.zs_r.at[way, step - 1, p], source)
-                    out = z_piece(s.z_out.at[way, step], p)
-                    out[...] = add(block[...], got[...])
-                    block = out
-                there = z_piece(s.z_in.at[way, step], p)
-                send(block, there, s.zs_s.at[way, step, p], s.zs_r.at[way, step, p], target)
-
-    def z_last():
-        for p in range(NP):
-            total = z_piece(s.part_image.at[z], p)[...].astype(F32)
-            for way in range(2):
-                got = z_piece(s.z_in.at[way, FAR], p)
-                source = (z_left, z_right)[way]
-                arrive(got, s.zs_s.at[way, FAR, p], s.zs_r.at[way, FAR, p], source)
-                total = total + got[...].astype(F32)
-            gi_out[PIECES[p][0], PIECES[p][1]] = total.astype(BF16)
+                z_take(way, steps)
+                total = total + s.z_in[way, steps].astype(F32)
+        gi_out[...] = total.astype(BF16)
 
     def grad_text(by):
         place = up(y, by)
@@ -454,48 +440,45 @@
         s.plane[place] = add(s.part_text[place, :, c], s.part_core[place])
 
     big_s = [
-        {
-            by: Scatter(
-                lambda o, q=up(x, by): s.plane.at[o, q, :, halves[0]],
-                s.big_in.at[0, up(x, by)], s.big_out.at[0, up(x, by)], y, at_y,
-                s.big_s_s.at[0, up(x, by)], s.big_s_r.at[0, up(x, by)], by % 2 == 0,
+        [
+            Scatter(
+                lambda o, q=up(x, by): s.plane.at[o, q, :, halves[0]], s.big_in.at[0, up(x, by)], y, at_y,
+                s.big_s_s.at[0, up(x, by)], s.big_s_r.at[0, up(x, by)],
             )
             for by in range(N)
-        },
-        {
-            by: Scatter(
-                lambda o, q=up(y, by): s.plane.at[q, o, :, halves[1]],
-                s.big_in.at[1, up(y, by)], s.big_out.at[1, up(y, by)], x, at_x,
-                s.big_s_s.at[1, up(y, by)], s.big_s_r.at[1, up(y, by)], by % 2 == 0,
+        ],
+        [
+            Scatter(
+                lambda o, q=up(y, by): s.plane.at[q, o, :, halves[1]], s.big_in.at[1, up(y, by)], x, at_x,
+                s.big_s_s.at[1, up(y, by)], s.big_s_r.at[1, up(y, by)],
             )
             for by in range(N)
-        },
+        ],
     ]
     small_s = [
-        Scatter(
-            lambda o: s.line.at[0, o], s.small_in.at[0], s.small_out.at[0], x, at_x,
-            s.small_s_s.at[0], s.small_s_r.at[0], True,
-        ),
-        Scatter(
-            lambda o: s.line.at[1, o], s.small_in.at[1], s.small_out.at[1], y, at_y,
-            s.small_s_s.at[1], s.small_s_r.at[1], True,
-        ),
+        Scatter(lambda o: s.line.at[0, o], s.small_in.at[0], x, at_x, s.small_s_s.at[0], s.small_s_r.at[0]),
+        Scatter(lambda o: s.line.at[1, o], s.small_in.at[1], y, at_y, s.small_s_s.at[1], s.small_s_r.at[1]),
     ]
 
     def fold(by):
         for h in range(2):
             q = up(x, by) if h == 0 else up(y, by)
-            s.line[h, q] = big_s[h][by].third()
+            s.line[h, q] = big_s[h][by].finish()
 
     grad_image(2)
-    z_scatter(1)
+    z_give(8, 2)
     grad_image(1)
     grad_image(3)
-    z_scatter(2)
+    z_give(7, 1)
+    z_give(5, -1)
+    z_give(4, 1)
     grad_image(0)
+    z_give(2, -1)
+    z_give(1, 1)
     for by in (2, 1, 3, 0):
         grad_text(by)
-    z_scatter(3)
+    for way in range(2):
+        z_hub(way, 6, (5, 7, 8))
 
     share_rows = jnp.sum(row_lse) * (1.0 / NZ)
     share_cols = jnp.sum(col_lse) * (1.0 / (N * N * CORES))
@@ -505,37 +488,24 @@
 
     for by in (2, 1, 3, 0):
         add_core(by)
-        big_s[1][by].first()
+        big_s[1][by].start()
     for by in (2, 1, 3, 0):
-        big_s[0][by].first()
-    z_scatter(4)
-    for by in (2, 1):
-        big_s[1][by].second()
-    z_scatter(5)
-    for by in (3, 0):
-        big_s[1][by].second()
+        big_s[0][by].start()
+    for way in range(2):
+        z_hub(way, 3, (2, 4, 6))
     s.loss2[y] = sum(collect(s.loss1, xc, N * CORES, at_xc, s.loss1_s, s.loss1_r))
     exchange(s.loss2, y, N, at_y, s.loss2_s, s.loss2_r)
     for by in (2, 1, 3, 0):
-        big_s[0][by].second()
-    z_scatter(6)
-    fold(2)
-    fold(1)
-    fold(3)
+        fold(by)
+    for h in range(2):
+        small_s[h].start()
     s.loss3[z] = sum(collect(s.loss2, y, N, at_y, s.loss2_s, s.loss2_r))
     exchange(s.loss3, z, NZ, at_z, s.loss3_s, s.loss3_r)
-    z_scatter(7)
     for h in range(2):
-        small_s[h].first()
-    fold(0)
-    z_scatter(8)
-    for h in range(2):
-        small_s[h].second()
-    for h in range(2):
-        gt_out[0, :, halves[h]] = small_s[h].third()
+        gt_out[0, :, halves[h]] = small_s[h].finish()
+    z_last()
     total = sum(collect(s.loss3, z, NZ, at_z, s.loss3_s, s.loss3_r))
     loss_out[0, 0] = jnp.max(total) / (2.0 * PAIRS)
-    z_last()
 
     for copy in sent:
         copy.wait_send()

time: 86.9 us -> 79.3 us (0.913)
  Pallas kernels: 80.1 us -> 73.1 us
    pallas_call x1, Pallas kernels: 80.1 us -> 73.1 us  [per_device(): pl.pallas_call(kernel, out_shape=(jax.ShapeDtypeStruct((1, 1), F32), jax....]
where the time goes in v3:
time: 79.3 us; the launch traced here: 78.4 us
  Pallas kernels  73.1 us (92%)
  local copies, waits for them, and re-layouts  2.93 us (4%)
  between operations  2.41 us (3%)
    pallas_call x1, Pallas kernels, per_device(): pl.pallas_call(kernel, out_shape=(jax.ShapeDtypeStruct((1, 1), F32), jax....  73.1 us
    unnamed x6, local copies, waits for them, and re-layouts  2.93 us

profile of v3, /device:TPU:24, one launch (start us, length us, event | category | flops | bytes accessed | tf_op | source)
XLA Modules:
  0.0 78.4 jit_solution(6250477631632170010)
XLA Ops:
  0.6 0.0 copy-start
  0.6 0.8 %copy-done = bf16[32,1024]{1,0:T(8,128)(2,1)S(1)} copy-done((bf16[32,1024]{1,0:T(8,128)(2,1)S(1)}, bf16[32,1024]{1,0:T(8,128)(2,1)}, u32[]{:S(2)}) %copy-start) | copy-done | bytes 65560
  1.5 0.0 copy-start.1
  1.5 0.8 %copy-done.1 = bf16[1,32,1024]{2,1,0:T(8,128)(2,1)S(1)} copy-done((bf16[1,32,1024]{2,1,0:T(8,128)(2,1)S(1)}, bf16[1,32,1024]{2,1,0:T(8,128)(2,1)}, u32[]{:S(2)}) %copy-start.1) | copy-done | bytes 65560
  2.3 73.1 %contrastive.1 = (f32[1,1]{1,0:T(1,128)}, bf16[32,1024]{1,0:T(8,128)(2,1)S(1)}, bf16[1,32,1024]{2,1,0:T(8,128)(2,1)S(1)}) custom-call(bf16[32,1024]{1,0:T(8,128)(2,1)S(1)} %copy-done, bf16[1,32,1024]{2,1,0:T(8,128)(2,1)S(1)} %copy-done.1), custom_call_target="tpu_custom_call" | custom-call | tf_op jit(solution)/shard_map/contrastive/pallas_call | solution.py:515
  76.0 0.6 copy.9
  76.7 0.6 copy.10
Async XLA Ops:
  0.6 0.8 %copy-start = (bf16[32,1024]{1,0:T(8,128)(2,1)S(1)}, bf16[32,1024]{1,0:T(8,128)(2,1)}, u32[]{:S(2)}) copy-start(bf16[32,1024]{1,0:T(8,128)(2,1)} %img_hbm.1) | copy-start | bytes 196612
  1.5 0.8 %copy-start.1 = (bf16[1,32,1024]{2,1,0:T(8,128)(2,1)S(1)}, bf16[1,32,1024]{2,1,0:T(8,128)(2,1)}, u32[]{:S(2)}) copy-start(bf16[1,32,1024]{2,1,0:T(8,128)(2,1)} %txt_hbm.1) | copy-start | bytes 196612

commit v4 on v3

--- a/solution.py
+++ b/solution.py
@@ -64,20 +64,18 @@
     loss2=f32(N, 1, 128),
     loss3=f32(NZ, 1, 128),
     local_sem=dma(2),
-    zg_s=dma(2, FAR + 1), zg_r=dma(2, FAR + 1),
-    small_g_s=dma(2, N), small_g_r=dma(2, N),
-    big_g_s=dma(2, N, N), big_g_r=dma(2, N, N),
-    core_g_s=dma(2, N), core_g_r=dma(2, N),
-    row1_s=dma(NZ), row1_r=dma(NZ),
-    col1_s=dma(N * CORES), col1_r=dma(N * CORES),
-    col2_s=dma(N), col2_r=dma(N),
-    loss1_s=dma(N * CORES), loss1_r=dma(N * CORES),
-    loss2_s=dma(N), loss2_r=dma(N),
-    loss3_s=dma(NZ), loss3_r=dma(NZ),
-    core_s_s=dma(N), core_s_r=dma(N),
-    zs_s=dma(2, FAR + 1), zs_r=dma(2, FAR + 1),
-    big_s_s=dma(2, N, N), big_s_r=dma(2, N, N),
-    small_s_s=dma(2, N), small_s_r=dma(2, N),
+    zg_s=dma(1), zg_r=dma(6),
+    text_s=dma(1), small_g_r=dma(2, N), big_g_r=dma(2, N),
+    core_g_s=dma(1), core_g_r=dma(1),
+    row1_s=dma(1), row1_r=dma(1),
+    col1_s=dma(1), col1_r=dma(1),
+    col2_s=dma(1), col2_r=dma(1),
+    loss1_s=dma(1), loss1_r=dma(1),
+    loss2_s=dma(1), loss2_r=dma(1),
+    loss3_s=dma(1), loss3_r=dma(1),
+    core_s_s=dma(1), core_s_r=dma(N),
+    zs_s=dma(1), zs_r=dma(5),
+    plane_s=dma(1), big_s_r=dma(2, N), small_s_r=dma(2),
 )
 NAMES = list(SCRATCH)
 
@@ -151,7 +149,6 @@
     )
     pl.semaphore_wait(barrier, len(partners))
 
-    sent = []
 
     def remote(src, dst, send_sem, recv_sem, device):
         return pltpu.make_async_remote_copy(
@@ -160,22 +157,18 @@
         )
 
     def send(*args):
-        copy = remote(*args)
-        copy.start()
-        sent.append(copy)
-
-    def arrive(dst, send_sem, recv_sem, device):
-        remote(dst, dst, send_sem, recv_sem, device).wait_recv()
+        remote(*args).start()
+
+    def wait_bytes(ref, sem):
+        pltpu.make_async_copy(ref, ref, sem).wait()
 
     def exchange(buf, me, count, device, ss, rs):
         for by in sorted(range(1, count), key=lambda k: -min(k, count - k)):
-            peer = up(me, by, count)
-            send(buf.at[me], buf.at[me], ss.at[by], rs.at[by], device(peer))
-
-    def collect(buf, me, count, device, ss, rs):
-        for by in sorted(range(1, count), key=lambda k: min(k, count - k)):
-            peer = up(me, -by, count)
-            arrive(buf.at[peer], ss.at[by], rs.at[by], device(peer))
+            send(buf.at[me], buf.at[me], ss.at[0], rs.at[0], device(up(me, by, count)))
+
+    def collect(buf, count, ss, rs):
+        wait_bytes(buf.at[pl.ds(0, count - 1)], rs.at[0])
+        wait_bytes(buf.at[pl.ds(0, count - 1)], ss.at[0])
         return [buf[j] for j in range(count)]
 
     class Gather:
@@ -185,11 +178,10 @@
         def start(self):
             own = self.slot(self.me)
             for by in (2, 1, 3):
-                send(own, own, self.ss.at[by], self.rs.at[by], self.device(up(self.me, by)))
+                send(own, own, self.ss, self.rs(by), self.device(up(self.me, by)))
 
         def wait(self, by):
-            origin = up(self.me, by)
-            arrive(self.slot(origin), self.ss.at[N - by], self.rs.at[N - by], self.device(origin))
+            wait_bytes(self.slot(up(self.me, by)), self.rs(N - by))
 
     class Scatter:
         def __init__(self, slot, r, me, device, ss, rs):
@@ -199,51 +191,47 @@
         def start(self):
             for by in (2, 1, 3):
                 to = up(self.me, by)
-                send(self.slot(to), self.r.at[by], self.ss.at[by], self.rs.at[by], self.device(to))
+                send(self.slot(to), self.r.at[by], self.ss, self.rs, self.device(to))
 
         def finish(self):
+            wait_bytes(self.r.at[pl.ds(1, 3)], self.rs)
             total = self.slot(self.me)[...].astype(F32)
             for by in (1, 3, 2):
-                arrive(self.r.at[by], self.ss.at[by], self.rs.at[by], self.device(up(self.me, -by)))
                 total = total + self.r[by].astype(F32)
             return total.astype(BF16)
 
-    upper, lower = pl.ds(0, ROWS // 2), pl.ds(ROWS // 2, ROWS // 2)
-    ends = (upper, lower)
+    ends = [pl.ds(0, ROWS // 2), pl.ds(ROWS // 2, ROWS // 2)]
 
     def along(way, steps):
         return at_z(up(z, steps if way == 0 else -steps, NZ))
 
-    def z_block(way, steps):
-        block = s.image.at[up(z, -steps if way == 0 else steps, NZ)]
-        return block.at[ends[way]] if steps == FAR else block
-
-    def z_send(way, held, reach):
-        block = s.image.at[up(z, -held if way == 0 else held, NZ)]
-        if reach == FAR:
-            block = block.at[ends[way]]
-        send(block, block, s.zg_s.at[way, reach], s.zg_r.at[way, reach], along(way, reach - held))
-
-    def z_wait(way, steps):
-        arrive(z_block(way, steps), s.zg_s.at[way, steps], s.zg_r.at[way, steps], along(way, -1))
+    def z_sem(way, reach):
+        return s.zg_r.at[{3: way, 6: 2 + way, 1: 4, 2: 4}.get(reach, 5)]
+
+    def z_send(way, held, reaches):
+        for reach in reaches:
+            block = s.image.at[up(z, -held if way == 0 else held, NZ)]
+            if reach == FAR:
+                block = block.at[ends[way]]
+            send(block, block, s.zg_s.at[0], z_sem(way, reach), along(way, reach - held))
 
     halves = [pl.ds(0, WIDE), pl.ds(WIDE, WIDE)]
     small_g = [
-        Gather(lambda o: s.text.at[y, o, c, :, halves[0]], x, at_x, s.small_g_s.at[0], s.small_g_r.at[0]),
-        Gather(lambda o: s.text.at[o, x, c, :, halves[1]], y, at_y, s.small_g_s.at[1], s.small_g_r.at[1]),
+        Gather(lambda o: s.text.at[y, o, c, :, halves[0]], x, at_x, s.text_s.at[0], lambda k: s.small_g_r.at[0, k]),
+        Gather(lambda o: s.text.at[o, x, c, :, halves[1]], y, at_y, s.text_s.at[0], lambda k: s.small_g_r.at[1, k]),
     ]
     big_g = [
         [
             Gather(
                 lambda o, q=up(x, by): s.text.at[o, q, c, :, halves[0]], y, at_y,
-                s.big_g_s.at[0, up(x, by)], s.big_g_r.at[0, up(x, by)],
+                s.text_s.at[0], lambda k, q=up(x, by): s.big_g_r.at[0, q],
             )
             for by in range(N)
         ],
         [
             Gather(
                 lambda o, q=up(y, by): s.text.at[q, o, c, :, halves[1]], x, at_x,
-                s.big_g_s.at[1, up(y, by)], s.big_g_r.at[1, up(y, by)],
+                s.text_s.at[0], lambda k, q=up(y, by): s.big_g_r.at[1, q],
             )
             for by in range(N)
         ],
@@ -256,16 +244,14 @@
 
     def share(by):
         for h in range(2):
-            for other in (1, 3, 2):
-                big_g[h][by].wait(other)
-            q = up(x, by) if h == 0 else up(y, by)
+            wait_bytes(s.line.at[h, pl.ds(0, 3)], s.big_g_r.at[h, up(x, by) if h == 0 else up(y, by)])
             block = core_block(h, by, c)
-            send(block, block, s.core_g_s.at[h, q], s.core_g_r.at[h, q], other_core)
+            send(block, block, s.core_g_s.at[0], s.core_g_r.at[0], other_core)
 
     own_image.wait()
     for reach in (3, 1):
         for way in range(2):
-            z_send(way, 0, reach)
+            z_send(way, 0, (reach,))
     own_text.wait()
     for h in range(2):
         small_g[h].start()
@@ -275,25 +261,19 @@
         for h in range(2):
             small_g[h].wait(by)
             big_g[h][by].start()
+    one = s.image.at[0]
     for way in range(2):
-        z_wait(way, 3)
-        for reach in (6, 4, 2):
-            z_send(way, 3, reach)
+        wait_bytes(one, z_sem(way, 3))
+        z_send(way, 3, (6, 4, 2))
     share(0)
+    for way in range(2):
+        wait_bytes(one, z_sem(way, 6))
+        z_send(way, 6, (8, 7, 5))
     share(1)
-    for way in range(2):
-        z_wait(way, 6)
-        for reach in (8, 7, 5):
-            z_send(way, 6, reach)
     share(3)
     share(2)
-    for by in (0, 1, 3, 2):
-        for h in range(2):
-            q = up(x, by) if h == 0 else up(y, by)
-            arrive(core_block(h, by, 1 - c), s.core_g_s.at[h, q], s.core_g_r.at[h, q], other_core)
-    for steps in (1, 2):
-        for way in range(2):
-            z_wait(way, steps)
+    wait_bytes(s.image, s.core_g_r.at[0])
+    wait_bytes(s.image.at[pl.ds(0, 4)], z_sem(0, 1))
 
     row_place = lax.broadcasted_iota(jnp.int32, (STRIP, COLS), 0)
 
@@ -340,29 +320,24 @@
         s.row_dense[q] = jnp.broadcast_to(dense, (8, 128))
 
     chunk_stats(0)
-    for steps in (4, 5, 7):
-        for way in range(2):
-            z_wait(way, steps)
+    wait_bytes(s.image.at[pl.ds(0, 7)], z_sem(0, 4))
 
     def near_chunk(k, carry):
-        chunk_stats(1 + 2 * k)
+        chunk_stats(1 + k)
         return carry
 
-    lax.fori_loop(0, 2, near_chunk, 0)
-    for way in range(2):
-        z_wait(way, FAR)
-    chunk_stats(2)
+    lax.fori_loop(0, 3, near_chunk, 0)
 
     s.row1[z] = jnp.concatenate([s.row_dense[j][0:1] for j in range(N)], axis=0)
     exchange(s.row1, z, NZ, at_z, s.row1_s, s.row1_r)
     col_local = log_sum([s.col_log[j] for j in range(N)])[0:1]
     s.col1[xc] = jnp.concatenate([col_local[:, j * 128 : (j + 1) * 128] for j in range(8)], axis=0)
     exchange(s.col1, xc, N * CORES, at_xc, s.col1_s, s.col1_r)
-    s.col2[y] = log_sum(collect(s.col1, xc, N * CORES, at_xc, s.col1_s, s.col1_r))
+    s.col2[y] = log_sum(collect(s.col1, N * CORES, s.col1_s, s.col1_r))
     exchange(s.col2, y, N, at_y, s.col2_s, s.col2_r)
-    col_lse = log_sum(collect(s.col2, y, N, at_y, s.col2_s, s.col2_r))
+    col_lse = log_sum(collect(s.col2, N, s.col2_s, s.col2_r))
     wide_col = jnp.concatenate([col_lse[j : j + 1] for j in range(8)], axis=1)
-    row_lse = log_sum(collect(s.row1, z, NZ, at_z, s.row1_s, s.row1_r))
+    row_lse = log_sum(collect(s.row1, NZ, s.row1_s, s.row1_r))
     on = eye()
     for j in range(N):
         spread = jnp.where(on, jnp.broadcast_to(row_lse[j : j + 1], (128, 128)), 0.0)
@@ -389,37 +364,33 @@
     def z_part(way, steps):
         return s.part_image.at[up(z, -steps if way == 0 else steps, NZ)]
 
+    def zs_sem(way, steps):
+        return s.zs_r.at[4 if steps in (1, 3) else (way if steps in (5, 7, 8) else 2 + way)]
+
     def z_give(steps, target):
         for way in range(2):
             block, there = z_part(way, steps), s.z_in.at[way, steps]
             if steps == FAR:
                 block, there = block.at[ends[way]], there.at[ends[way]]
-            send(block, there, s.zs_s.at[way, steps], s.zs_r.at[way, steps], along(way, -target))
-
-    def z_take(way, steps):
-        got = s.z_in.at[way, steps]
-        if steps == FAR:
-            got = got.at[ends[way]]
-        arrive(got, s.zs_s.at[way, steps], s.zs_r.at[way, steps], along(way, 1))
+            send(block, there, s.zs_s.at[0], zs_sem(way, steps), along(way, -target))
 
     def z_hub(way, steps, parts):
-        total = z_part(way, steps)[...].astype(F32)
-        for part in parts:
-            z_take(way, part)
-        for part in parts:
-            if part != FAR:
-                total = total + s.z_in[way, part].astype(F32)
+        waited = s.image.at[pl.ds(0, 5), ends[0]] if FAR in parts else s.image.at[pl.ds(0, 3)]
+        wait_bytes(waited, zs_sem(way, parts[0]))
         out = s.z_out.at[way, steps // 3 - 1]
-        out[...] = total.astype(BF16)
-        if FAR in parts:
-            out[ends[way]] = (total[ends[way].start : ends[way].start + ends[way].size] + s.z_in[way, FAR, ends[way]].astype(F32)).astype(BF16)
-        send(out, s.z_in.at[way, steps], s.zs_s.at[way, steps], s.zs_r.at[way, steps], along(way, -3))
+        for p in range(2):
+            total = z_part(way, steps)[ends[p]].astype(F32)
+            for part in parts:
+                if part != FAR or p == way:
+                    total = total + s.z_in[way, part, ends[p]].astype(F32)
+            out[ends[p]] = total.astype(BF16)
+        send(out, s.z_in.at[way, steps], s.zs_s.at[0], zs_sem(way, steps), along(way, -3))
 
     def z_last():
+        wait_bytes(s.image.at[pl.ds(0, 4)], zs_sem(0, 1))
         total = s.part_image[z].astype(F32)
         for steps in (1, 3):
             for way in range(2):
-                z_take(way, steps)
                 total = total + s.z_in[way, steps].astype(F32)
         gi_out[...] = total.astype(BF16)
 
@@ -432,32 +403,32 @@
             w, s.image[...].reshape(NZ * ROWS, D), (((0,), (0,)), ((), ())), preferred_element_type=F32
         )
         s.part_text[place] = out.astype(BF16).reshape(N, CORES, ROWS, D)
-        send(s.part_text.at[place, :, 1 - c], s.part_core.at[place], s.core_s_s.at[by], s.core_s_r.at[by], other_core)
+        send(s.part_text.at[place, :, 1 - c], s.part_core.at[place], s.core_s_s.at[0], s.core_s_r.at[by], other_core)
 
     def add_core(by):
         place = up(y, by)
-        arrive(s.part_core.at[place], s.core_s_s.at[by], s.core_s_r.at[by], other_core)
+        wait_bytes(s.part_core.at[place], s.core_s_r.at[by])
         s.plane[place] = add(s.part_text[place, :, c], s.part_core[place])
 
     big_s = [
         [
             Scatter(
                 lambda o, q=up(x, by): s.plane.at[o, q, :, halves[0]], s.big_in.at[0, up(x, by)], y, at_y,
-                s.big_s_s.at[0, up(x, by)], s.big_s_r.at[0, up(x, by)],
+                s.plane_s.at[0], s.big_s_r.at[0, up(x, by)],
             )
             for by in range(N)
         ],
         [
             Scatter(
                 lambda o, q=up(y, by): s.plane.at[q, o, :, halves[1]], s.big_in.at[1, up(y, by)], x, at_x,
-                s.big_s_s.at[1, up(y, by)], s.big_s_r.at[1, up(y, by)],
+                s.plane_s.at[0], s.big_s_r.at[1, up(y, by)],
             )
             for by in range(N)
         ],
     ]
     small_s = [
-        Scatter(lambda o: s.line.at[0, o], s.small_in.at[0], x, at_x, s.small_s_s.at[0], s.small_s_r.at[0]),
-        Scatter(lambda o: s.line.at[1, o], s.small_in.at[1], y, at_y, s.small_s_s.at[1], s.small_s_r.at[1]),
+        Scatter(lambda o: s.line.at[0, o], s.small_in.at[0], x, at_x, s.plane_s.at[0], s.small_s_r.at[0]),
+        Scatter(lambda o: s.line.at[1, o], s.small_in.at[1], y, at_y, s.plane_s.at[0], s.small_s_r.at[1]),
     ]
 
     def fold(by):
@@ -474,17 +445,15 @@
     z_give(4, 1)
     grad_image(0)
     z_give(2, -1)
-    z_give(1, 1)
     for by in (2, 1, 3, 0):
         grad_text(by)
-    for way in range(2):
-        z_hub(way, 6, (5, 7, 8))
+    z_give(1, 1)
 
     share_rows = jnp.sum(row_lse) * (1.0 / NZ)
     share_cols = jnp.sum(col_lse) * (1.0 / (N * N * CORES))
     own_share = share_rows + share_cols - 2.0 * jnp.sum(s.diag[...])
-    s.loss1[xc] = jnp.full((1, 128), own_share, F32)
-    exchange(s.loss1, xc, N * CORES, at_xc, s.loss1_s, s.loss1_r)
+    s.loss3[z] = jnp.full((1, 128), own_share, F32)
+    exchange(s.loss3, z, NZ, at_z, s.loss3_s, s.loss3_r)
 
     for by in (2, 1, 3, 0):
         add_core(by)
@@ -492,23 +461,28 @@
     for by in (2, 1, 3, 0):
         big_s[0][by].start()
     for way in range(2):
-        z_hub(way, 3, (2, 4, 6))
-    s.loss2[y] = sum(collect(s.loss1, xc, N * CORES, at_xc, s.loss1_s, s.loss1_r))
-    exchange(s.loss2, y, N, at_y, s.loss2_s, s.loss2_r)
+        z_hub(way, 6, (5, 7, 8))
+    s.loss1[xc] = sum(collect(s.loss3, NZ, s.loss3_s, s.loss3_r))
+    exchange(s.loss1, xc, N * CORES, at_xc, s.loss1_s, s.loss1_r)
     for by in (2, 1, 3, 0):
         fold(by)
     for h in range(2):
         small_s[h].start()
-    s.loss3[z] = sum(collect(s.loss2, y, N, at_y, s.loss2_s, s.loss2_r))
-    exchange(s.loss3, z, NZ, at_z, s.loss3_s, s.loss3_r)
+    for way in range(2):
+        z_hub(way, 3, (2, 4, 6))
+    s.loss2[y] = sum(collect(s.loss1, N * CORES, s.loss1_s, s.loss1_r))
+    exchange(s.loss2, y, N, at_y, s.loss2_s, s.loss2_r)
     for h in range(2):
         gt_out[0, :, halves[h]] = small_s[h].finish()
+    total = sum(collect(s.loss2, N, s.loss2_s, s.loss2_r))
+    loss_out[0, 0] = jnp.max(total) / (2.0 * PAIRS)
     z_last()
-    total = sum(collect(s.loss3, z, NZ, at_z, s.loss3_s, s.loss3_r))
-    loss_out[0, 0] = jnp.max(total) / (2.0 * PAIRS)
-
-    for copy in sent:
-        copy.wait_send()
+
+    fifteen = s.image.at[pl.ds(0, NZ - 1)]
+    for sem in (s.zg_s, s.text_s, s.zs_s, s.plane_s):
+        wait_bytes(fifteen, sem.at[0])
+    for sem in (s.core_g_s, s.core_s_s):
+        wait_bytes(s.image, sem.at[0])
 
 
 def per_device(images, texts):
@@ -527,7 +501,7 @@
         ),
         scratch_shapes=list(SCRATCH.values()),
         compiler_params=pltpu.CompilerParams(
-            collective_id=0, has_side_effects=True, vmem_limit_bytes=48 * 1024 * 1024
+            collective_id=0, has_side_effects=True, vmem_limit_bytes=60 * 1024 * 1024
         ),
         name="contrastive",
     )(images, texts)

time: 79.3 us -> 73.6 us (0.928)
  Pallas kernels: 73.1 us -> 67.7 us
    pallas_call x1, Pallas kernels: 73.1 us -> 67.7 us  [per_device(): pl.pallas_call(kernel, out_shape=(jax.ShapeDtypeStruct((1, 1), F32), jax....]
    unnamed x6 -> x4, local copies, waits for them, and re-layouts: 2.93 us -> 2.14 us
where the time goes in v4:
time: 73.6 us; the launch traced here: 72.3 us
  Pallas kernels  67.7 us (92%)
  between operations  2.4 us (3%)
  local copies, waits for them, and re-layouts  2.14 us (3%)
    pallas_call x1, Pallas kernels, per_device(): pl.pallas_call(kernel, out_shape=(jax.ShapeDtypeStruct((1, 1), F32), jax....  67.7 us
    unnamed x4, local copies, waits for them, and re-layouts  2.14 us

profile of v4, /device:TPU:24, one launch (start us, length us, event | category | flops | bytes accessed | tf_op | source)
XLA Modules:
  0.0 72.3 jit_solution(10708249861492949295)
XLA Ops:
  0.6 67.7 %contrastive.1 = (f32[1,1]{1,0:T(1,128)}, bf16[32,1024]{1,0:T(8,128)(2,1)}, bf16[1,32,1024]{2,1,0:T(8,128)(2,1)}) custom-call(bf16[32,1024]{1,0:T(8,128)(2,1)} %img_hbm.1, bf16[1,32,1024]{2,1,0:T(8,128)(2,1)} %txt_hbm.1), custom_call_target="tpu_custom_call" | custom-call | tf_op jit(solution)/shard_map/contrastive/pallas_call | solution.py:489
  69.0 0.0 copy-start
  69.0 1.5 %copy.9 = bf16[32,1024]{1,0:T(8,128)(2,1)} copy(bf16[32,1024]{1,0:T(8,128)(2,1)} %get-tuple-element.13) | data formatting | bytes 131072
  70.5 0.0 copy-done
  70.5 0.6 copy.10
Async XLA Ops:
  69.0 1.5 %copy-start = (bf16[1,32,1024]{2,1,0:T(8,128)(2,1)S(1)}, bf16[1,32,1024]{2,1,0:T(8,128)(2,1)}, u32[]{:S(2)}) copy-start(bf16[1,32,1024]{2,1,0:T(8,128)(2,1)} %get-tuple-element.14) | copy-start | bytes 196612

commit v5 on v4

--- a/solution.py
+++ b/solution.py
@@ -22,6 +22,8 @@
 STRIP = ROWS
 FAR = NZ // 2
 
+PLACES = [0, 1, -1, 3, -3, 2, -2, 4, -4, 6, -6, 5, -5, 7, -7, 8]
+
 def dma(*shape):
     return pltpu.SemaphoreType.DMA(shape)
 
@@ -41,8 +43,7 @@
     col_exp=f32(N, CHUNK, COLS),
     row_peak=f32(N, CHUNK, 128),
     row_scale=f32(N, CHUNK, 128),
-    row_log=f32(CHUNK, 128),
-    row_dense=f32(N, 8, 128),
+    row_dense=f32(N, 128),
     col_peak=f32(N, 8, COLS),
     col_log=f32(N, 8, COLS),
     col_ids=pltpu.VMEM((8, COLS), jnp.int32),
@@ -64,7 +65,7 @@
     loss2=f32(N, 1, 128),
     loss3=f32(NZ, 1, 128),
     local_sem=dma(2),
-    zg_s=dma(1), zg_r=dma(6),
+    zg_s=dma(1), zg_r=dma(7),
     text_s=dma(1), small_g_r=dma(2, N), big_g_r=dma(2, N),
     core_g_s=dma(1), core_g_r=dma(1),
     row1_s=dma(1), row1_r=dma(1),
@@ -96,17 +97,11 @@
     return peak + jnp.log(total)
 
 
-def eye():
-    rows = lax.broadcasted_iota(jnp.int32, (128, 128), 0)
-    cols = lax.broadcasted_iota(jnp.int32, (128, 128), 1)
-    return rows == cols
-
-
 def add(a, b):
     return (a.astype(F32) + b.astype(F32)).astype(BF16)
 
 
-def kernel(img_hbm, txt_hbm, loss_out, gi_out, gt_out, *refs):
+def kernel(img_hbm, txt_hbm, loss_out, both_out, *refs):
     s = Refs(refs)
     img, txt = lax.axis_index("img"), lax.axis_index("txt")
     y, zl = img // N, lax.rem(img, N)
@@ -131,7 +126,7 @@
 
     other_core = (img, (zh * N + x) * CORES + (1 - c))
 
-    own_image = pltpu.make_async_copy(img_hbm, s.image.at[z], s.local_sem.at[0])
+    own_image = pltpu.make_async_copy(img_hbm, s.image.at[0], s.local_sem.at[0])
     own_text = pltpu.make_async_copy(txt_hbm.at[0], s.text.at[y, x, c], s.local_sem.at[1])
     own_image.start()
     own_text.start()
@@ -206,14 +201,17 @@
         return at_z(up(z, steps if way == 0 else -steps, NZ))
 
     def z_sem(way, reach):
-        return s.zg_r.at[{3: way, 6: 2 + way, 1: 4, 2: 4}.get(reach, 5)]
+        return s.zg_r.at[{3: way, 6: 2 + way, 1: 4, 2: 5, 4: 5}.get(reach, 6)]
+
+    def slot(way, steps):
+        return PLACES.index(steps if way == 1 or steps == FAR else -steps)
 
     def z_send(way, held, reaches):
         for reach in reaches:
-            block = s.image.at[up(z, -held if way == 0 else held, NZ)]
+            block, there = s.image.at[slot(way, held)], s.image.at[slot(way, reach)]
             if reach == FAR:
-                block = block.at[ends[way]]
-            send(block, block, s.zg_s.at[0], z_sem(way, reach), along(way, reach - held))
+                block, there = block.at[ends[way]], there.at[ends[way]]
+            send(block, there, s.zg_s.at[0], z_sem(way, reach), along(way, reach - held))
 
     halves = [pl.ds(0, WIDE), pl.ds(WIDE, WIDE)]
     small_g = [
@@ -268,24 +266,37 @@
     share(0)
     for way in range(2):
         wait_bytes(one, z_sem(way, 6))
-        z_send(way, 6, (8, 7, 5))
+        z_send(way, 6, (5, 7, 8))
     share(1)
     share(3)
     share(2)
     wait_bytes(s.image, s.core_g_r.at[0])
-    wait_bytes(s.image.at[pl.ds(0, 4)], z_sem(0, 1))
 
     row_place = lax.broadcasted_iota(jnp.int32, (STRIP, COLS), 0)
 
-    def diagonal(q, strip):
-        first = y * 4096 + strip * 1024 + (q * N + x) * 64 + c * 32
+    def origin(g, strip):
+        o = up(z, PLACES[g * N + strip], NZ)
+        return o // N, lax.rem(o, N)
+
+    def diagonal(g, strip):
+        q, r = origin(g, strip)
+        first = y * 4096 + r * 1024 + (q * N + x) * 64 + c * 32
         return row_place + first == s.col_ids[0:1, :]
 
+    def in_lanes(g, strip):
+        _, r = origin(g, strip)
+        rows = lax.broadcasted_iota(jnp.int32, (STRIP, 128), 0)
+        return rows + r * ROWS == lax.broadcasted_iota(jnp.int32, (STRIP, 128), 1)
+
+    def in_rows(g, strip):
+        q, _ = origin(g, strip)
+        return lax.broadcasted_iota(jnp.int32, (N, 128), 0) == q
+
+    s.row_dense[...] = jnp.zeros((N, 128), F32)
     s.diag[...] = jnp.zeros((8, 128), F32)
 
-    def chunk_stats(by):
-        q = lax.rem(zh + by, N)
-        images = s.image[pl.ds(q * N, N)].reshape(CHUNK, D)
+    def chunk_stats(q):
+        images = s.image[q * N : (q + 1) * N].reshape(CHUNK, D)
         s.col_exp[q] = LOGIT_SCALE * lax.dot_general(
             images, s.text[...].reshape(COLS, D), (((1,), (1,)), ((), ())), preferred_element_type=F32
         )
@@ -298,7 +309,8 @@
             s.row_exp[q, rows, :] = exps
             s.row_peak[q, rows, :] = jnp.broadcast_to(peak, (STRIP, 128))
             log = peak + jnp.log(jnp.sum(exps, axis=1, keepdims=True))
-            s.row_log[rows, :] = jnp.broadcast_to(log, (STRIP, 128))
+            dense = jnp.sum(jnp.where(in_lanes(q, strip), log, 0.0), axis=0, keepdims=True)
+            s.row_dense[...] += jnp.where(in_rows(q, strip), dense, 0.0)
             part = jnp.max(logits.reshape(STRIP // 8, 8, COLS), axis=0)
             col_peak = part if col_peak is None else jnp.maximum(col_peak, part)
         col_peak = jnp.max(col_peak, axis=0, keepdims=True)
@@ -316,19 +328,16 @@
         s.col_peak[q] = jnp.broadcast_to(col_peak, (8, COLS))
         col_log = col_peak + jnp.log(jnp.sum(col_total, axis=0, keepdims=True))
         s.col_log[q] = jnp.broadcast_to(col_log, (8, COLS))
-        dense = jnp.sum(jnp.where(eye(), s.row_log[...], 0.0), axis=0, keepdims=True)
-        s.row_dense[q] = jnp.broadcast_to(dense, (8, 128))
-
+
+    wait_bytes(s.image.at[pl.ds(0, 2)], z_sem(0, 1))
     chunk_stats(0)
-    wait_bytes(s.image.at[pl.ds(0, 7)], z_sem(0, 4))
-
-    def near_chunk(k, carry):
-        chunk_stats(1 + k)
-        return carry
-
-    lax.fori_loop(0, 3, near_chunk, 0)
-
-    s.row1[z] = jnp.concatenate([s.row_dense[j][0:1] for j in range(N)], axis=0)
+    wait_bytes(s.image.at[pl.ds(0, 4)], z_sem(0, 2))
+    chunk_stats(1)
+    wait_bytes(s.image.at[pl.ds(0, 5)], z_sem(0, 5))
+    chunk_stats(2)
+    chunk_stats(3)
+
+    s.row1[z] = s.row_dense[...]
     exchange(s.row1, z, NZ, at_z, s.row1_s, s.row1_r)
     col_local = log_sum([s.col_log[j] for j in range(N)])[0:1]
     s.col1[xc] = jnp.concatenate([col_local[:, j * 128 : (j + 1) * 128] for j in range(8)], axis=0)
@@ -338,13 +347,14 @@
     col_lse = log_sum(collect(s.col2, N, s.col2_s, s.col2_r))
     wide_col = jnp.concatenate([col_lse[j : j + 1] for j in range(8)], axis=1)
     row_lse = log_sum(collect(s.row1, NZ, s.row1_s, s.row1_r))
-    on = eye()
-    for j in range(N):
-        spread = jnp.where(on, jnp.broadcast_to(row_lse[j : j + 1], (128, 128)), 0.0)
-        column = jnp.sum(spread, axis=1, keepdims=True)
-        s.row_scale[j] = (0.5 * LOGIT_SCALE) * jnp.exp(s.row_peak[j] - column)
-
-    def chunk_weights(q, carry):
+    for j in range(NZ):
+        g, strip = j // N, j % N
+        rows = slice(strip * STRIP, (strip + 1) * STRIP)
+        lanes = jnp.sum(jnp.where(in_rows(g, strip), row_lse, 0.0), axis=0, keepdims=True)
+        column = jnp.sum(jnp.where(in_lanes(g, strip), lanes, 0.0), axis=1, keepdims=True)
+        s.row_scale[g, rows, :] = (0.5 * LOGIT_SCALE) * jnp.exp(s.row_peak[g, rows, :] - column)
+
+    def chunk_weights(q):
         col_scale = (0.5 * LOGIT_SCALE) * jnp.exp(s.col_peak[q, 0:1, :] - wide_col)
         for strip in range(N):
             rows = slice(strip * STRIP, (strip + 1) * STRIP)
@@ -352,17 +362,16 @@
             value = s.row_exp[q, rows, :] * row_scale + s.col_exp[q, rows, :] * col_scale
             value = value - jnp.where(diagonal(q, strip), LOGIT_SCALE, 0.0)
             s.weights[q, rows, :] = value.astype(BF16)
-        return carry
-
-    lax.fori_loop(0, N, chunk_weights, 0)
-
-    def grad_image(by):
-        q = up(zh, by)
-        out = jnp.dot(s.weights[q], s.text[...].reshape(COLS, D), preferred_element_type=F32)
-        s.part_image[pl.ds(q * N, N)] = out.astype(BF16).reshape(N, ROWS, D)
+
+    for g in (3, 2, 1, 0):
+        chunk_weights(g)
+
+    def grad_image(g):
+        out = jnp.dot(s.weights[g], s.text[...].reshape(COLS, D), preferred_element_type=F32)
+        s.part_image[g * N : (g + 1) * N] = out.astype(BF16).reshape(N, ROWS, D)
 
     def z_part(way, steps):
-        return s.part_image.at[up(z, -steps if way == 0 else steps, NZ)]
+        return s.part_image.at[slot(way, steps)]
 
     def zs_sem(way, steps):
         return s.zs_r.at[4 if steps in (1, 3) else (way if steps in (5, 7, 8) else 2 + way)]
@@ -388,11 +397,11 @@
 
     def z_last():
         wait_bytes(s.image.at[pl.ds(0, 4)], zs_sem(0, 1))
-        total = s.part_image[z].astype(F32)
+        total = s.part_image[0].astype(F32)
         for steps in (1, 3):
             for way in range(2):
                 total = total + s.z_in[way, steps].astype(F32)
-        gi_out[...] = total.astype(BF16)
+        both_out[0] = total.astype(BF16)
 
     def grad_text(by):
         place = up(y, by)
@@ -436,15 +445,15 @@
             q = up(x, by) if h == 0 else up(y, by)
             s.line[h, q] = big_s[h][by].finish()
 
+    grad_image(3)
+    z_give(8, 2)
+    z_give(7, 1)
     grad_image(2)
-    z_give(8, 2)
+    z_give(5, -1)
     grad_image(1)
-    grad_image(3)
-    z_give(7, 1)
-    z_give(5, -1)
     z_give(4, 1)
+    z_give(2, -1)
     grad_image(0)
-    z_give(2, -1)
     for by in (2, 1, 3, 0):
         grad_text(by)
     z_give(1, 1)
@@ -473,7 +482,7 @@
     s.loss2[y] = sum(collect(s.loss1, N * CORES, s.loss1_s, s.loss1_r))
     exchange(s.loss2, y, N, at_y, s.loss2_s, s.loss2_r)
     for h in range(2):
-        gt_out[0, :, halves[h]] = small_s[h].finish()
+        both_out[1, :, halves[h]] = small_s[h].finish()
     total = sum(collect(s.loss2, N, s.loss2_s, s.loss2_r))
     loss_out[0, 0] = jnp.max(total) / (2.0 * PAIRS)
     z_last()
@@ -486,17 +495,15 @@
 
 
 def per_device(images, texts):
-    loss, grad_images, grad_texts = pl.pallas_call(
+    loss, both = pl.pallas_call(
         kernel,
         out_shape=(
             jax.ShapeDtypeStruct((1, 1), F32),
-            jax.ShapeDtypeStruct((ROWS, D), BF16),
-            jax.ShapeDtypeStruct((1, ROWS, D), BF16),
+            jax.ShapeDtypeStruct((2, ROWS, D), BF16),
         ),
         in_specs=[pl.BlockSpec(memory_space=pl.ANY)] * 2,
         out_specs=(
             pl.BlockSpec(memory_space=pltpu.SMEM),
-            pl.BlockSpec(memory_space=pltpu.VMEM),
             pl.BlockSpec(memory_space=pltpu.VMEM),
         ),
         scratch_shapes=list(SCRATCH.values()),
@@ -505,7 +512,7 @@
         ),
         name="contrastive",
     )(images, texts)
-    return loss.reshape(()), grad_images, grad_texts
+    return loss.reshape(()), both[0], both[1:2]
 
 
 def solution(mesh):

time: 73.6 us -> 73.6 us (level)
  the two profiles are of different devices: /device:TPU:24 before, /device:TPU:1 now
where the time goes in v5:
time: 73.6 us; the launch traced here: 73.4 us
  Pallas kernels  69.5 us (94%)
  between operations  2.39 us (3%)
  local copies, waits for them, and re-layouts  1.53 us (2%)
    pallas_call x1, Pallas kernels, per_device(): pl.pallas_call(kernel, out_shape=(jax.ShapeDtypeStruct((1, 1), F32), jax....  69.5 us
    slice x1, local copies, waits for them, and re-layouts, per_device(): return (loss.reshape(()), both[0], both[1:2])  1.53 us

profile of v5, /device:TPU:1, one launch (start us, length us, event | category | flops | bytes accessed | tf_op | source)
XLA Modules:
  0.0 73.4 jit_solution(9895944421381822196)
XLA Ops:
  0.6 69.5 %contrastive.1 = (f32[1,1]{1,0:T(1,128)}, bf16[2,32,1024]{2,1,0:T(8,128)(2,1)}) custom-call(bf16[32,1024]{1,0:T(8,128)(2,1)} %img_hbm.1, bf16[1,32,1024]{2,1,0:T(8,128)(2,1)} %txt_hbm.1), custom_call_target="tpu_custom_call" | custom-call | tf_op jit(solution)/shard_map/contrastive/pallas_call | solution.py:498
  70.2 1.5 %fusion = (bf16[1,32,1024]{2,1,0:T(8,128)(2,1)}, bf16[32,1024]{1,0:T(8,128)(2,1)}) fusion(bf16[2,32,1024]{2,1,0:T(8,128)(2,1)} %get-tuple-element.6), kind=kLoop, calls=%fused_computation.1 | loop fusion | bytes 262144 | tf_op jit(solution)/shard_map/slice | solution.py:515

commit v6 on v5

--- a/solution.py
+++ b/solution.py
@@ -445,6 +445,12 @@
             q = up(x, by) if h == 0 else up(y, by)
             s.line[h, q] = big_s[h][by].finish()
 
+    share_rows = jnp.sum(row_lse) * (1.0 / NZ)
+    share_cols = jnp.sum(col_lse) * (1.0 / (N * N * CORES))
+    own_share = share_rows + share_cols - 2.0 * jnp.sum(s.diag[...])
+    s.loss3[z] = jnp.full((1, 128), own_share, F32)
+    exchange(s.loss3, z, NZ, at_z, s.loss3_s, s.loss3_r)
+
     grad_image(3)
     z_give(8, 2)
     z_give(7, 1)
@@ -457,12 +463,6 @@
     for by in (2, 1, 3, 0):
         grad_text(by)
     z_give(1, 1)
-
-    share_rows = jnp.sum(row_lse) * (1.0 / NZ)
-    share_cols = jnp.sum(col_lse) * (1.0 / (N * N * CORES))
-    own_share = share_rows + share_cols - 2.0 * jnp.sum(s.diag[...])
-    s.loss3[z] = jnp.full((1, 128), own_share, F32)
-    exchange(s.loss3, z, NZ, at_z, s.loss3_s, s.loss3_r)
 
     for by in (2, 1, 3, 0):
         add_core(by)

time: 73.6 us -> 69.5 us (0.944)
  the two profiles are of different devices: /device:TPU:1 before, /device:TPU:24 now
where the time goes in v6:
time: 69.5 us; the launch traced here: 69.3 us
  Pallas kernels  65.4 us (94%)
  between operations  2.39 us (3%)
  local copies, waits for them, and re-layouts  1.53 us (2%)
    pallas_call x1, Pallas kernels, per_device(): pl.pallas_call(kernel, out_shape=(jax.ShapeDtypeStruct((1, 1), F32), jax....  65.4 us
    slice x1, local copies, waits for them, and re-layouts, per_device(): return (loss.reshape(()), both[0], both[1:2])  1.53 us

profile of v6, /device:TPU:24, one launch (start us, length us, event | category | flops | bytes accessed | tf_op | source)
XLA Modules:
  0.0 69.3 jit_solution(641125209435412978)
XLA Ops:
  0.6 65.4 %contrastive.1 = (f32[1,1]{1,0:T(1,128)}, bf16[2,32,1024]{2,1,0:T(8,128)(2,1)}) custom-call(bf16[32,1024]{1,0:T(8,128)(2,1)} %img_hbm.1, bf16[1,32,1024]{2,1,0:T(8,128)(2,1)} %txt_hbm.1), custom_call_target="tpu_custom_call" | custom-call | tf_op jit(solution)/shard_map/contrastive/pallas_call | solution.py:498
  66.0 1.5 %fusion = (bf16[1,32,1024]{2,1,0:T(8,128)(2,1)}, bf16[32,1024]{1,0:T(8,128)(2,1)}) fusion(bf16[2,32,1024]{2,1,0:T(8,128)(2,1)} %get-tuple-element.6), kind=kLoop, calls=%fused_computation.1 | loop fusion | bytes 262144 | tf_op jit(solution)/shard_map/slice | solution.py:515

commit v7 on v6

--- a/solution.py
+++ b/solution.py
@@ -161,9 +161,8 @@
         for by in sorted(range(1, count), key=lambda k: -min(k, count - k)):
             send(buf.at[me], buf.at[me], ss.at[0], rs.at[0], device(up(me, by, count)))
 
-    def collect(buf, count, ss, rs):
+    def collect(buf, count, rs):
         wait_bytes(buf.at[pl.ds(0, count - 1)], rs.at[0])
-        wait_bytes(buf.at[pl.ds(0, count - 1)], ss.at[0])
         return [buf[j] for j in range(count)]
 
     class Gather:
@@ -342,11 +341,11 @@
     col_local = log_sum([s.col_log[j] for j in range(N)])[0:1]
     s.col1[xc] = jnp.concatenate([col_local[:, j * 128 : (j + 1) * 128] for j in range(8)], axis=0)
     exchange(s.col1, xc, N * CORES, at_xc, s.col1_s, s.col1_r)
-    s.col2[y] = log_sum(collect(s.col1, N * CORES, s.col1_s, s.col1_r))
+    s.col2[y] = log_sum(collect(s.col1, N * CORES, s.col1_r))
     exchange(s.col2, y, N, at_y, s.col2_s, s.col2_r)
-    col_lse = log_sum(collect(s.col2, N, s.col2_s, s.col2_r))
+    col_lse = log_sum(collect(s.col2, N, s.col2_r))
     wide_col = jnp.concatenate([col_lse[j : j + 1] for j in range(8)], axis=1)
-    row_lse = log_sum(collect(s.row1, NZ, s.row1_s, s.row1_r))
+    row_lse = log_sum(collect(s.row1, NZ, s.row1_r))
     for j in range(NZ):
         g, strip = j // N, j % N
         rows = slice(strip * STRIP, (strip + 1) * STRIP)
@@ -471,7 +470,7 @@
         big_s[0][by].start()
     for way in range(2):
         z_hub(way, 6, (5, 7, 8))
-    s.loss1[xc] = sum(collect(s.loss3, NZ, s.loss3_s, s.loss3_r))
+    s.loss1[xc] = sum(collect(s.loss3, NZ, s.loss3_r))
     exchange(s.loss1, xc, N * CORES, at_xc, s.loss1_s, s.loss1_r)
     for by in (2, 1, 3, 0):
         fold(by)
@@ -479,14 +478,18 @@
         small_s[h].start()
     for way in range(2):
         z_hub(way, 3, (2, 4, 6))
-    s.loss2[y] = sum(collect(s.loss1, N * CORES, s.loss1_s, s.loss1_r))
+    s.loss2[y] = sum(collect(s.loss1, N * CORES, s.loss1_r))
     exchange(s.loss2, y, N, at_y, s.loss2_s, s.loss2_r)
     for h in range(2):
         both_out[1, :, halves[h]] = small_s[h].finish()
-    total = sum(collect(s.loss2, N, s.loss2_s, s.loss2_r))
+    total = sum(collect(s.loss2, N, s.loss2_r))
     loss_out[0, 0] = jnp.max(total) / (2.0 * PAIRS)
     z_last()
 
+    tiles = ((s.row1, s.row1_s), (s.col1, s.col1_s), (s.col2, s.col2_s))
+    tiles += ((s.loss1, s.loss1_s), (s.loss2, s.loss2_s), (s.loss3, s.loss3_s))
+    for buf, sem in tiles:
+        wait_bytes(buf.at[pl.ds(0, buf.shape[0] - 1)], sem.at[0])
     fifteen = s.image.at[pl.ds(0, NZ - 1)]
     for sem in (s.zg_s, s.text_s, s.zs_s, s.plane_s):
         wait_bytes(fifteen, sem.at[0])

time: 69.5 us -> 69.5 us (level)
  no operation moved by 1% of the time
where the time goes in v7:
time: 69.5 us; the launch traced here: 69.3 us
  Pallas kernels  65.4 us (94%)
  between operations  2.39 us (3%)
  local copies, waits for them, and re-layouts  1.53 us (2%)
    pallas_call x1, Pallas kernels, per_device(): pl.pallas_call(kernel, out_shape=(jax.ShapeDtypeStruct((1, 1), F32), jax....  65.4 us
    slice x1, local copies, waits for them, and re-layouts, per_device(): return (loss.reshape(()), both[0], both[1:2])  1.53 us

profile of v7, /device:TPU:24, one launch (start us, length us, event | category | flops | bytes accessed | tf_op | source)
XLA Modules:
  0.0 69.3 jit_solution(8650112216153828544)
XLA Ops:
  0.6 65.4 %contrastive.1 = (f32[1,1]{1,0:T(1,128)}, bf16[2,32,1024]{2,1,0:T(8,128)(2,1)}) custom-call(bf16[32,1024]{1,0:T(8,128)(2,1)} %img_hbm.1, bf16[1,32,1024]{2,1,0:T(8,128)(2,1)} %txt_hbm.1), custom_call_target="tpu_custom_call" | custom-call | tf_op jit(solution)/shard_map/contrastive/pallas_call | solution.py:501
  66.1 1.5 %fusion = (bf16[1,32,1024]{2,1,0:T(8,128)(2,1)}, bf16[32,1024]{1,0:T(8,128)(2,1)}) fusion(bf16[2,32,1024]{2,1,0:T(8,128)(2,1)} %get-tuple-element.6), kind=kLoop, calls=%fused_computation.1 | loop fusion | bytes 262144 | tf_op jit(solution)/shard_map/slice | solution.py:518

commit v8 on v7

--- a/solution.py
+++ b/solution.py
@@ -352,6 +352,12 @@
         lanes = jnp.sum(jnp.where(in_rows(g, strip), row_lse, 0.0), axis=0, keepdims=True)
         column = jnp.sum(jnp.where(in_lanes(g, strip), lanes, 0.0), axis=1, keepdims=True)
         s.row_scale[g, rows, :] = (0.5 * LOGIT_SCALE) * jnp.exp(s.row_peak[g, rows, :] - column)
+    share_rows = jnp.sum(row_lse) * (1.0 / NZ)
+    share_cols = jnp.sum(col_lse) * (1.0 / (N * N * CORES))
+    own_share = share_rows + share_cols - 2.0 * jnp.sum(s.diag[...])
+    s.loss3[z] = jnp.full((1, 128), own_share, F32)
+    exchange(s.loss3, z, NZ, at_z, s.loss3_s, s.loss3_r)
+
 
     def chunk_weights(q):
         col_scale = (0.5 * LOGIT_SCALE) * jnp.exp(s.col_peak[q, 0:1, :] - wide_col)
@@ -443,12 +449,6 @@
         for h in range(2):
             q = up(x, by) if h == 0 else up(y, by)
             s.line[h, q] = big_s[h][by].finish()
-
-    share_rows = jnp.sum(row_lse) * (1.0 / NZ)
-    share_cols = jnp.sum(col_lse) * (1.0 / (N * N * CORES))
-    own_share = share_rows + share_cols - 2.0 * jnp.sum(s.diag[...])
-    s.loss3[z] = jnp.full((1, 128), own_share, F32)
-    exchange(s.loss3, z, NZ, at_z, s.loss3_s, s.loss3_r)
 
     grad_image(3)
     z_give(8, 2)

time: 69.5 us -> 69.4 us (level)
  no operation moved by 1% of the time
where the time goes in v8:
time: 69.4 us; the launch traced here: 69.2 us
  Pallas kernels  65.3 us (94%)
  between operations  2.39 us (3%)
  local copies, waits for them, and re-layouts  1.53 us (2%)
    pallas_call x1, Pallas kernels, per_device(): pl.pallas_call(kernel, out_shape=(jax.ShapeDtypeStruct((1, 1), F32), jax....  65.3 us
    slice x1, local copies, waits for them, and re-layouts, per_device(): return (loss.reshape(()), both[0], both[1:2])  1.53 us

profile of v8, /device:TPU:24, one launch (start us, length us, event | category | flops | bytes accessed | tf_op | source)
XLA Modules:
  0.0 69.2 jit_solution(5064185932504627818)
XLA Ops:
  0.6 65.3 %contrastive.1 = (f32[1,1]{1,0:T(1,128)}, bf16[2,32,1024]{2,1,0:T(8,128)(2,1)}) custom-call(bf16[32,1024]{1,0:T(8,128)(2,1)} %img_hbm.1, bf16[1,32,1024]{2,1,0:T(8,128)(2,1)} %txt_hbm.1), custom_call_target="tpu_custom_call" | custom-call | tf_op jit(solution)/shard_map/contrastive/pallas_call | solution.py:501
  66.0 1.5 %fusion = (bf16[1,32,1024]{2,1,0:T(8,128)(2,1)}, bf16[32,1024]{1,0:T(8,128)(2,1)}) fusion(bf16[2,32,1024]{2,1,0:T(8,128)(2,1)} %get-tuple-element.6), kind=kLoop, calls=%fused_computation.1 | loop fusion | bytes 262144 | tf_op jit(solution)/shard_map/slice | solution.py:518
